TPU v7x, 128 devices: a whole 4x4x4 slice. The times are simulated.
128 devices in a mesh: seq: 8 (over y_lo, x), dp: 16 (over z, y_hi, core).
Axes of the slice: x: 4, y: 4 (y_hi: 2, y_lo: 2; y = y_hi * 2 + y_lo), z: 4, core: 2. Of those that a mesh axis runs over, the one named last changes fastest.
Arguments:
- inputs: float32 [16, 2048, 768], P('dp', 'seq'), may hold values from -6 to 6
- routes: int32 [16, 2048, 2], P('dp', 'seq'), may hold values from 0 to 15, all different within a row; in each aligned block of 256 rows (0 to 255, 256 to 511, ..., all dimensions but the last counted through in order) at most 40 rows name the same one
- buckets: int32 [2048], replicated, may hold values from 0 to 31, as said below
- norm1_gain: bfloat16 [768], P(('seq', 'dp')), may hold values from 0.5 to 1.5
- qkv_weight: bfloat16 [768, 2304], P(('seq', 'dp')), may hold values from -0.3125 to 0.3125
- out_weight: bfloat16 [768, 768], P(('seq', 'dp')), may hold values from -0.875 to 0.875
- rel_bias: bfloat16 [384], P(('seq', 'dp')), may hold values from -3 to 3
- norm2_gain: bfloat16 [768], P(('seq', 'dp')), may hold values from 0.5 to 1.5
- router_projection_weight: bfloat16 [768, 16], P(('seq', 'dp')), may hold values from -0.15625 to 0.15625
- expert_in: bfloat16 [16, 768, 3072], P('dp', None, 'seq'), may hold values from -0.21875 to 0.21875
- expert_out: bfloat16 [16, 3072, 768], P('dp', 'seq'), may hold values from -0.15625 to 0.15625
- cotangent: float32 [16, 2048, 768], P('dp', 'seq'), may hold values from -6 to 6
Outputs:
- layer_out: float32 [16, 2048, 768], P('dp', 'seq')
- input_grad: float32 [16, 2048, 768], P('dp', 'seq')
- norm1_grad: float32 [768], P(('seq', 'dp'))
- qkv_grad: float32 [768, 2304], P(('seq', 'dp'))
- out_grad: float32 [768, 768], P(('seq', 'dp'))
- bias_grad: float32 [384], P(('seq', 'dp'))
- norm2_grad: float32 [768], P(('seq', 'dp'))
- router_grad: float32 [768, 16], P(('seq', 'dp'))
- expert_in_grad: float32 [16, 768, 3072], P('dp', None, 'seq')
- expert_out_grad: float32 [16, 3072, 768], P('dp', 'seq')
Inputs may be any that keep to these rules, and one draw needn't show every extreme that they name: `routes`: in the rows of one sequence on one device (aligned blocks of 256 token rows) no expert is named more than 40 times, a bound that some block reaches; a token's two experts differ. `buckets`: the bucket never falls as the distance grows; each distance below 16 has a bucket of its own, and the largest distance has bucket 32 - 1.
All inputs are finite; a program needn't handle non-finite values.
Results may differ from a plain program's by a relative error of at most 0.025.
Values may be sent and summed in bfloat16 or wider, within the bound.
No kernel may reach another device: no remote copies, remote signals or barrier semaphores. Data moves between devices by JAX's collectives and lax.ppermute only.
A program may use at most 256 MiB of HBM per device.

v0:
```python
import math

import jax
import jax.numpy as jnp
from jax import lax
from jax.sharding import Mesh
from jax.sharding import PartitionSpec as P

D = 768
HEADS = 12
HEAD_DIM = 64
BUCKETS = 32
DP = ("dp_0", "dp_1", "dp_2")
SEQ_DP = ("seq_0", "seq_1", "dp_0", "dp_1", "dp_2")
SEQ = ("seq_0", "seq_1")


def side_by_side(arrays, axis, dim, along):
    columns = [a.reshape(*a.shape[:along], -1) for a in arrays]
    both = jnp.concatenate(columns, axis=along)
    filled, at, done = (lax.all_gather(both, axis, axis=dim, tiled=True), 0, [])
    for a, column in zip(arrays, columns):
        slab = filled[..., at : at + column.shape[along]]
        done.append(slab.reshape(*slab.shape[:along], *a.shape[along:]))
        at += column.shape[along]
    return tuple(done)


def gather_turned(arrays, axis, dims):
    turned = [jnp.moveaxis(a, dim, 0) for a, dim in zip(arrays, dims)]
    widths = [t[0].size for t in turned]
    both = jnp.concatenate([t.reshape(-1, w) for t, w in zip(turned, widths)], axis=1)
    filled = lax.all_gather(both, axis, axis=0, tiled=True)
    blocks = jnp.split(filled, [sum(widths[:k]) for k in range(1, len(widths))], axis=1)
    return tuple(
        (
            jnp.moveaxis(b.reshape(-1, *t.shape[1:]), 0, dim)
            for b, t, dim in zip(blocks, turned, dims)
        )
    )


def split_up(value, dim, size):
    shape = value.shape
    blocks = value.reshape(*shape[:dim], size, shape[dim] // size, *shape[dim + 1 :])
    return jnp.moveaxis(blocks, dim, 0)


def sum_by_chip(value, chips, core, dim):
    sizes = (lax.axis_size(chips), lax.axis_size(core))
    blocks = split_up(value, dim, sizes[0] * sizes[1])
    inside = blocks.shape[1:]
    blocks = blocks.reshape(*sizes, *inside).swapaxes(0, 1).reshape(-1, *inside)
    blocks = lax.psum_scatter(blocks, core, scatter_dimension=0, tiled=True)
    return lax.psum_scatter(blocks, chips, scatter_dimension=0, tiled=True)[0]


def normalize(values):
    multiplier = lax.rsqrt(jnp.mean(values * values, axis=-1, keepdims=True) + 1e-06)
    return (values * multiplier, multiplier)


def norm_back(grad_normed, normed, multiplier):
    return multiplier * (
        grad_normed - normed * jnp.mean(grad_normed * normed, axis=-1, keepdims=True)
    )


def gelu_slope(values):
    return (
        0.5 * (1.0 + lax.erf(values * 0.7071067811865476))
        + values * jnp.exp(-0.5 * values * values) * 0.3989422804014327
    )


def shards(
    inputs,
    routes,
    buckets,
    norm1_gain,
    qkv_weight,
    out_weight,
    rel_bias,
    norm2_gain,
    router_projection_weight,
    expert_in,
    expert_out,
    cotangent,
):
    num_seqs = inputs.shape[0]
    seq_rows = inputs.shape[1]
    length = buckets.shape[0]
    experts = lax.axis_size(DP)
    capacity = max(2, 10 * seq_rows // (4 * experts))
    slot_count = num_seqs * capacity
    routed_rows = experts * slot_count
    tokens = num_seqs * seq_rows
    score_scale = 1.0 / math.sqrt(HEAD_DIM)
    fetched = (
        *side_by_side((norm1_gain, qkv_weight, out_weight), SEQ_DP, 0, 1),
        lax.all_gather(rel_bias, SEQ_DP, axis=0, tiled=True),
        *side_by_side((norm2_gain, router_projection_weight), SEQ_DP, 0, 1),
    )
    gain_one = fetched[0].astype(jnp.float32)
    qkv_full = fetched[1]
    out_full = fetched[2]
    relative_bias_lookup = fetched[3].reshape(HEADS, BUCKETS)
    gain_two = fetched[4].astype(jnp.float32)
    router_full = fetched[5]
    flat_in = inputs.reshape(tokens, D)
    normed_one, factor_one = normalize(flat_in)
    h_one = (normed_one * gain_one).astype(jnp.bfloat16)
    qkv = (
        jnp.dot(h_one, qkv_full, preferred_element_type=jnp.float32)
        .astype(jnp.bfloat16)
        .reshape(num_seqs, seq_rows, 3 * D)
    )
    queries = qkv[:, :, :D].reshape(num_seqs, seq_rows, HEADS, HEAD_DIM)
    kv_all = lax.all_gather(qkv[:, :, D:], SEQ, axis=1, tiled=True)
    key_rows = kv_all[:, :, :D].reshape(num_seqs, length, HEADS, HEAD_DIM)
    value_rows = kv_all[:, :, D:].reshape(num_seqs, length, HEADS, HEAD_DIM)
    bucket_range = jnp.arange(BUCKETS, dtype=jnp.int32)
    bucket_starts = jnp.sum((buckets[:, None] < bucket_range[None, :]).astype(jnp.int32), axis=0)
    bucket_ends = jnp.concatenate([bucket_starts[1:], jnp.full((1,), length, jnp.int32)])
    first_query = lax.axis_index(SEQ) * seq_rows
    distance = (
        first_query
        + jnp.arange(seq_rows, dtype=jnp.int32)[:, None]
        - jnp.arange(length, dtype=jnp.int32)[None, :]
    )
    causal = distance >= 0
    clipped = jnp.clip(distance, 0, length - 1)
    bucket_onehot_matrix = (
        (clipped[None] >= bucket_starts[:, None, None])
        & (clipped[None] < bucket_ends[:, None, None])
    ).astype(jnp.bfloat16)
    position_bias = jnp.einsum(
        "aei,pa->pei",
        bucket_onehot_matrix,
        relative_bias_lookup,
        preferred_element_type=jnp.float32,
    )

    def scores_of():
        raw_scores = (
            jnp.einsum("sqhd,skhd->shqk", queries, key_rows, preferred_element_type=jnp.float32)
            * score_scale
        )
        return jnp.where(causal[None, None], raw_scores + position_bias[None], -1e30)

    scores = scores_of()
    row_max = jnp.max(scores, axis=-1, keepdims=True)
    expd = jnp.exp(scores - row_max)
    row_total = jnp.sum(expd, axis=-1, keepdims=True)
    probs = expd / row_total
    log_total = row_max + jnp.log(row_total)
    attended = jnp.einsum(
        "shqk,skhd->sqhd",
        probs.astype(jnp.bfloat16),
        value_rows,
        preferred_element_type=jnp.float32,
    )
    attended = attended.reshape(tokens, D).astype(jnp.bfloat16)
    middle = flat_in + jnp.dot(attended, out_full, preferred_element_type=jnp.float32)
    normed_two, factor_two = normalize(middle)
    h_two = (normed_two * gain_two).astype(jnp.bfloat16)
    logits = jnp.dot(h_two, router_full, preferred_element_type=jnp.float32)
    route_pairs = routes.reshape(tokens, 2)
    route_onehot = (
        route_pairs[:, :, None] == jnp.arange(experts, dtype=jnp.int32)[None, None, :]
    ).astype(jnp.float32)
    chosen = jnp.sum(logits[:, None, :] * route_onehot, axis=-1)
    gate_values = jax.nn.softmax(chosen, axis=1)
    flat_onehot = route_onehot.reshape(tokens * 2, experts)
    earlier = jnp.cumsum(flat_onehot, axis=0) - flat_onehot
    slot_index = jnp.sum(earlier * flat_onehot, axis=-1).astype(jnp.int32)
    target = route_pairs.reshape(tokens * 2) * slot_count + slot_index
    dispatch_map = (target[:, None] == jnp.arange(routed_rows, dtype=jnp.int32)[None, :]).astype(
        jnp.bfloat16
    )
    token_map = jnp.sum(dispatch_map.reshape(tokens, 2, routed_rows), axis=1)
    outgoing = jnp.einsum("tc,td->cd", token_map, h_two, preferred_element_type=jnp.float32).astype(
        jnp.bfloat16
    )
    arrived = lax.all_to_all(
        outgoing.reshape(experts, slot_count, D), DP, split_axis=0, concat_axis=0, tiled=True
    ).reshape(routed_rows, D)
    full_in, full_out = gather_turned((expert_in, expert_out), SEQ, (2, 1))
    weight_in = full_in[0]
    weight_out = full_out[0]
    preact = jnp.dot(arrived, weight_in, preferred_element_type=jnp.float32)
    activated = jax.nn.gelu(preact, approximate=False).astype(jnp.bfloat16)
    produced = jnp.dot(activated, weight_out, preferred_element_type=jnp.float32).astype(
        jnp.bfloat16
    )
    returned = lax.all_to_all(
        produced.reshape(experts, slot_count, D), DP, split_axis=0, concat_axis=0, tiled=True
    ).reshape(routed_rows, D)
    picked = jnp.dot(dispatch_map, returned, preferred_element_type=jnp.float32).reshape(
        tokens, 2, D
    )
    layer_out = middle + jnp.sum(gate_values[:, :, None] * picked, axis=1)
    grad_out = cotangent.reshape(tokens, D)
    grad_gates = jnp.sum(grad_out[:, None, :] * picked, axis=-1)
    grad_chosen = gate_values * (
        grad_gates - jnp.sum(gate_values * grad_gates, axis=1, keepdims=True)
    )
    router_logit_gradient = jnp.sum(grad_chosen[:, :, None] * route_onehot, axis=1)
    grad_assign = (
        (gate_values[:, :, None] * grad_out[:, None, :]).reshape(tokens * 2, D).astype(jnp.bfloat16)
    )
    outgoing_grad = jnp.einsum(
        "ac,ad->cd", dispatch_map, grad_assign, preferred_element_type=jnp.float32
    ).astype(jnp.bfloat16)
    incoming_gradient = lax.all_to_all(
        outgoing_grad.reshape(experts, slot_count, D), DP, split_axis=0, concat_axis=0, tiled=True
    ).reshape(routed_rows, D)
    slope = gelu_slope(preact)
    grad_act = jnp.einsum(
        "rd,fd->rf", incoming_gradient, weight_out, preferred_element_type=jnp.float32
    )
    grad_preact = (grad_act * slope).astype(jnp.bfloat16)
    grad_weight_out = jnp.einsum(
        "rf,rd->fd", activated, incoming_gradient, preferred_element_type=jnp.float32
    )
    grad_weight_in = jnp.einsum(
        "rd,rf->df", arrived, grad_preact, preferred_element_type=jnp.float32
    )
    grad_rows = jnp.einsum(
        "rf,df->rd", grad_preact, weight_in, preferred_element_type=jnp.float32
    ).astype(jnp.bfloat16)
    in_shard, out_shard = (
        lax.psum_scatter(
            grad_weight_in[None].astype(jnp.bfloat16), SEQ, scatter_dimension=2, tiled=True
        ).astype(jnp.float32),
        lax.psum_scatter(
            grad_weight_out[None].astype(jnp.bfloat16), SEQ, scatter_dimension=1, tiled=True
        ).astype(jnp.float32),
    )
    grad_back = lax.all_to_all(
        grad_rows.reshape(experts, slot_count, D), DP, split_axis=0, concat_axis=0, tiled=True
    ).reshape(routed_rows, D)
    router_float = router_full.astype(jnp.float32)
    grad_h_two = jnp.dot(token_map, grad_back, preferred_element_type=jnp.float32)
    grad_h_two = grad_h_two + jnp.dot(
        router_logit_gradient, router_float.T, precision=lax.Precision.HIGHEST
    )
    grad_router = jnp.dot(
        h_two.astype(jnp.float32).T, router_logit_gradient, precision=lax.Precision.HIGHEST
    )
    grad_gain_two = jnp.sum(grad_h_two * normed_two, axis=0)
    grad_middle = grad_out + norm_back(grad_h_two * gain_two, normed_two, factor_two)
    grad_branch = grad_middle.astype(jnp.bfloat16)
    grad_out_weight = jnp.einsum(
        "td,te->de", attended, grad_branch, preferred_element_type=jnp.float32
    )
    grad_attended = jnp.einsum(
        "te,de->td", grad_branch, out_full, preferred_element_type=jnp.float32
    )
    grad_attended = grad_attended.astype(jnp.bfloat16).reshape(num_seqs, seq_rows, HEADS, HEAD_DIM)
    probs_again = jnp.exp(scores_of() - log_total)
    grad_probs = jnp.einsum(
        "sqhd,skhd->shqk", grad_attended, value_rows, preferred_element_type=jnp.float32
    )
    row_inner = jnp.sum(probs_again * grad_probs, axis=-1, keepdims=True)
    score_gradient = (probs_again * (grad_probs - row_inner)).astype(jnp.bfloat16)
    grad_queries = (
        jnp.einsum("shqk,skhd->sqhd", score_gradient, key_rows, preferred_element_type=jnp.float32)
        * score_scale
    )
    key_gradient = (
        jnp.einsum("shqk,sqhd->skhd", score_gradient, queries, preferred_element_type=jnp.float32)
        * score_scale
    )
    grad_values = jnp.einsum(
        "shqk,sqhd->skhd",
        probs_again.astype(jnp.bfloat16),
        grad_attended,
        preferred_element_type=jnp.float32,
    )
    kv_terms = jnp.concatenate(
        [key_gradient.reshape(num_seqs, length, D), grad_values.reshape(num_seqs, length, D)],
        axis=-1,
    )
    grad_kv = lax.psum_scatter(
        kv_terms.astype(jnp.bfloat16), SEQ, scatter_dimension=1, tiled=True
    ).astype(jnp.float32)
    grad_qkv = jnp.concatenate([grad_queries.reshape(num_seqs, seq_rows, D), grad_kv], axis=-1)
    grad_qkv = grad_qkv.reshape(tokens, 3 * D).astype(jnp.bfloat16)
    grad_table = jnp.einsum(
        "ojta,zta->jz", score_gradient, bucket_onehot_matrix, preferred_element_type=jnp.float32
    ).reshape(HEADS * BUCKETS)
    grad_qkv_weight = jnp.einsum("td,te->de", h_one, grad_qkv, preferred_element_type=jnp.float32)
    grad_h_one = jnp.einsum("te,de->td", grad_qkv, qkv_full, preferred_element_type=jnp.float32)
    grad_gain_one = jnp.sum(grad_h_one * normed_one, axis=0)
    input_grad = grad_middle + norm_back(grad_h_one * gain_one, normed_one, factor_one)
    summed = (
        sum_by_chip(grad_gain_one, ("seq_0", "seq_1", "dp_0", "dp_1"), "dp_2", 0),
        sum_by_chip(grad_qkv_weight, ("seq_0", "seq_1", "dp_0", "dp_1"), "dp_2", 0),
        sum_by_chip(grad_out_weight, ("seq_0", "seq_1", "dp_0", "dp_1"), "dp_2", 0),
        sum_by_chip(grad_table, ("seq_0", "seq_1", "dp_0", "dp_1"), "dp_2", 0),
        sum_by_chip(grad_gain_two, ("seq_0", "seq_1", "dp_0", "dp_1"), "dp_2", 0),
        sum_by_chip(grad_router, ("seq_0", "seq_1", "dp_0", "dp_1"), "dp_2", 0),
    )
    return (
        layer_out.reshape(num_seqs, seq_rows, D),
        input_grad.reshape(num_seqs, seq_rows, D),
        summed[0],
        summed[1],
        summed[2],
        summed[3],
        summed[4],
        summed[5],
        in_shard,
        out_shard,
    )


def solution(mesh):
    torus = Mesh(mesh.devices.reshape(2, 4, 4, 2, 2), ("seq_0", "seq_1", "dp_0", "dp_1", "dp_2"))
    in_specs = (
        P(DP, SEQ, None),
        P(DP, SEQ, None),
        P(),
        P(SEQ_DP),
        P(SEQ_DP, None),
        P(SEQ_DP, None),
        P(SEQ_DP),
        P(SEQ_DP),
        P(SEQ_DP, None),
        P(DP, None, SEQ),
        P(DP, SEQ, None),
        P(DP, SEQ, None),
    )
    out_specs = (
        P(DP, SEQ, None),
        P(DP, SEQ, None),
        P(SEQ_DP),
        P(SEQ_DP, None),
        P(SEQ_DP, None),
        P(SEQ_DP),
        P(SEQ_DP),
        P(SEQ_DP, None),
        P(DP, None, SEQ),
        P(DP, SEQ, None),
    )
    return jax.shard_map(
        shards, mesh=torus, in_specs=in_specs, out_specs=out_specs, check_vma=False
    )
```

profile of v0, /device:TPU:0, one launch (start us, length us, event | category | flops | bytes accessed | tf_op | source)
XLA Modules:
  0.0 1551.1 jit_solution(16282970005381610688)
XLA Ops:
  10.9 203.6 %all-gather.10.cloned.1.call-done = bf16[128,6,3073]{2,1,0:T(8,128)(2,1)} async-done(((bf16[1,6,3073]{2,1,0:T(8,128)(2,1)}), bf16[128,6,3073]{2,1,0:T(8,128)(2,1)}) %all-gather.10.cloned.1.call-update) | async-done | bytes 4720144 | tf_op jit(solution)/shard_map/all_gather | solution.py:21
  214.5 9.9 reshape.537
  238.5 16.4 %compare_and_fusion = pred[32,256,2048]{1,0,2:T(32,128)(4,1)} fusion(s32[256,2048]{0,1:T(8,128)} %copy.187, s32[32]{0:T(128)S(1)} %pad_add_fusion, s32[32]{0:T(128)S(1)} %convert_reduce_fusion.2), kind=kLoop, calls=%fused_computation | loop fusion | flops 50331648 | bytes 18874624 | tf_op jit(solution)/shard_map/and | solution.py:134
  254.9 89.9 %copy.188 = pred[32,256,2048]{2,0,1:T(32,128)(4,1)} copy(pred[32,256,2048]{1,0,2:T(32,128)(4,1)} %compare_and_fusion) | data formatting | bytes 33554432 | tf_op jit(solution)/shard_map/and | solution.py:134
  345.1 105.8 %all-reduce = bf16[384]{0:T(512)(128)(2,1)S(1)} all-reduce(bf16[384]{0:T(512)(128)(2,1)S(1)} %dynamic-update-slice), channel_id=1, replica_groups=mesh['seq_0'=2,'seq_1'=4,'dp_0'=4,'dp_1'=2,'dp_2'=2] {'seq_0','seq_1','d..., use_global_device_ids=true, to_apply=%add | all-reduce | flops 384 | bytes 1536
  451.2 174.3 %all-gather.1 = bf16[128,6,17]{2,1,0:T(8,128)(2,1)S(1)} all-gather(bf16[1,6,17]{2,1,0:T(8,128)(2,1)S(1)} %maximum_bitcast_fusion.4), channel_id=1, replica_groups=mesh['seq_0'=2,'seq_1'=4,'dp_0'=4,'dp_1'=2,'dp_2'=2] {'seq_0','seq_1','d..., dimensions={0}, use_global_device_ids=true | all-gather | bytes 26316 | tf_op jit(solution)/shard_map/all_gather | solution.py:21
  632.2 18.6 %fusion.81 = f32[12,256,2048]{2,0,1:T(8,128)} fusion(bf16[12,32,1]{1,0,2:T(8,128)(2,1)S(1)} %reshape.540, pred[32,256,2048]{2,0,1:T(32,128)(4,1)} %copy.188), kind=kOutput, calls=%fused_computation.165 | convolution fusion | flops 402653184 | bytes 41943808 | tf_op jit(solution)/shard_map/aei,pa->pei/dot_general | solution.py:137
  666.4 29.6 %fusion.80 = (f32[12,256]{1,0:T(8,128)S(1)}, f32[12,256,2048]{2,1,0:T(8,128)}) fusion(f32[12,256,2048]{2,0,1:T(8,128)} %fusion.81, bf16[256,12,64]{0,2,1:T(8,128)(2,1)S(1)} %bitcast.220, bf16[2048,12,64]{0,2,1:T(8,128)(2,1)} %bitcast.211, pred[256,2048]{1,0:T(8,128)(4,1)S(1)} %fusion.38), kind=kOutput, calls=%fused_computation.164 | convolution fusion | flops 830469120 | bytes 54407168 | tf_op jit(solution)/shard_map/sqhd,skhd->shqk/dot_general | solution.py:146
  696.0 10.6 fusion.1
  706.6 10.6 fusion.48
  729.5 13.3 all-to-all-done
  747.5 22.5 %fusion.9 = (bf16[640,3072]{1,0:T(8,128)(2,1)S(1)}, f32[640,3072]{1,0:T(8,128)}) fusion(bf16[640,768]{1,0:T(8,128)(2,1)} %bitcast.16, bf16[3072,1536]{1,0:T(8,128)(2,1)} %all-gather.8.cloned.1.call-done), kind=kOutput, calls=%fused_computation.17 | convolution fusion | flops 3147694080 | bytes 17498112 | tf_op jit(solution)/shard_map/dot_general | solution.py:191
  776.1 7.3 all-to-all-start.1
  783.4 8.0 fusion.15
  793.5 6.6 fusion.42
  801.7 6.6 all-to-all-start.3
  811.6 13.9 all-to-all-done.3
  832.7 16.5 %multiply_reduce_fusion = (f32[12,256]{1,0:T(8,128)S(1)}, f32[12,256,2048]{2,1,0:T(8,128)}) fusion(f32[12,256,2048]{2,1,0:T(8,128)} %get-tuple-element.28, f32[12,256]{1,0:T(8,128)S(1)} %log_add_fusion, bf16[256,12,64]{0,2,1:T(8,128)(2,1)S(1)} %bitcast.223, bf16[2048,12,64]{0,2,1:T(8,128)(2,1)} %bitcast.216), kind=kOutput, calls=%fused_computation.4 | convolution fusion | flops 824177664 | bytes 53895168 | tf_op jit(solution)/shard_map/sqhd,skhd->shqk/dot_general | solution.py:262
  849.2 12.0 fusion.31
  861.2 16.6 %multiply_convert_fusion = bf16[12,256,2048]{2,1,0:T(8,128)(2,1)S(1)} fusion(f32[12,256,2048]{2,1,0:T(8,128)} %get-tuple-element.35, f32[12,256,2048]{2,1,0:T(8,128)} %get-tuple-element.28, f32[12,256]{1,0:T(8,128)S(1)} %get-tuple-element.34, f32[12,256]{1,0:T(8,128)S(1)} %log_add_fusion), kind=kLoop, calls=%fused_computation.3 | loop fusion | flops 25165824 | bytes 62939136 | tf_op jit(solution)/shard_map/convert_element_type | solution.py:266
  899.9 8.5 fusion.47
  908.8 53.5 %reduce-scatter.25.cloned.1.call-done = bf16[1,256,1536]{2,1,0:T(8,128)(2,1)} async-done(((bf16[1,2048,1536]{2,1,0:T(8,128)(2,1)}), bf16[1,256,1536]{2,1,0:T(8,128)(2,1)}) %reduce-scatter.25.cloned.1.call-update) | async-done | bytes 786448 | tf_op jit(solution)/shard_map/reduce_scatter | solution.py:285
  973.3 23.4 %copy.212 = bf16[12,256,2048]{1,0,2:T(8,128)(2,1)} copy(bf16[12,256,2048]{2,1,0:T(8,128)(2,1)} %copy-done) | data formatting | bytes 25165824 | tf_op jit(solution)/shard_map/convert_element_type | solution.py:266
  996.7 14.7 convolution_bitcast_fusion.3
  1015.6 8.5 fusion.23
  1024.1 20.4 %copy.240 = bf16[1,768,3072]{1,0,2:T(2,128)(2,1)} copy(bf16[1,768,3072]{2,1,0:T(8,128)(2,1)} %fusion.23) | data formatting | bytes 9437184
  1044.5 6.7 copy.270
  1051.3 8.4 fusion.24
  1065.3 46.0 %reduce-scatter.41.cloned.1.call-done = bf16[384,768]{1,0:T(8,128)(2,1)} async-done(((bf16[3072,768]{1,0:T(8,128)(2,1)}), bf16[384,768]{1,0:T(8,128)(2,1)}) %reduce-scatter.41.cloned.1.call-update) | async-done | bytes 589840
  1118.1 52.5 %reduce-scatter.31.cloned.1.call-done = bf16[1,384,768]{2,1,0:T(8,128)(2,1)} async-done(((bf16[1,3072,768]{2,1,0:T(8,128)(2,1)}), bf16[1,384,768]{2,1,0:T(8,128)(2,1)}) %reduce-scatter.31.cloned.1.call-update) | async-done | bytes 589840 | tf_op jit(solution)/shard_map/reduce_scatter | solution.py:236
  1174.5 7.7 reduce-scatter.33.cloned.1.call-done
  1182.9 353.2 %all-reduce.7 = (f32[64,6]{0,1:T(8,128)S(1)}, f32[64,3]{0,1:T(4,128)S(1)}, f32[64,6]{0,1:T(8,128)S(1)}, f32[64,6,16]{2,1,0:T(8,128)S(1)}) all-reduce(f32[64,6]{0,1:T(8,128)S(1)} %copy.223, f32[64,3]{0,1:T(4,128)S(1)} %copy.231, ...), channel_id=4, replica_groups=mesh['seq_0'=2,'seq_1'=4,'dp_0'=4,'dp_1'=2,'dp_2'=2] {'seq_0','seq_1','d..., use_global_device_ids=true, to_apply=%region_22.23.clone | all-reduce | flops 7104 | bytes 56832
  (239 shorter events, 140.0 us)
Async XLA Ops:
  7.2 218.9 %copy-start.6 = (f32[1,256,768]{2,1,0:T(8,128)S(1)}, f32[1,256,768]{2,1,0:T(8,128)}, u32[]{:S(2)}) copy-start(f32[1,256,768]{2,1,0:T(8,128)} %param.12) | copy-start | bytes 2359300
  7.2 207.3 %all-gather.10.cloned.1.call-start = ((), (), s32[]{:S(2)}) async-start(), calls=%async_computation.19 | async-start | bytes 6604800 | tf_op jit(solution)/shard_map/all_gather | solution.py:21
  9.6 641.5 %all-gather.6.cloned.1.call-start = ((), (), s32[]{:S(2)}) async-start(), calls=%async_computation.13 | async-start | bytes 7077888 | tf_op jit(solution)/shard_map/all_gather | solution.py:119
  10.9 218.8 %copy-start.28 = (f32[256]{0:T(256)}, f32[256]{0:T(256)S(1)}, u32[]{:S(2)}) copy-start(f32[256]{0:T(256)S(1)} %add_rsqrt_fusion.1) | copy-start | bytes 3076
  10.9 220.8 %copy-start.17 = (bf16[1,768,384]{2,1,0:T(8,128)(2,1)S(1)}, bf16[1,768,384]{2,1,0:T(8,128)(2,1)}, u32[]{:S(2)}) copy-start(bf16[1,768,384]{2,1,0:T(8,128)(2,1)} %param.21) | copy-start | bytes 1769476
  231.6 515.9 %all-gather.8.cloned.1.call-start = ((), (), s32[]{:S(2)}) async-start(), calls=%async_computation.14 | async-start | bytes 10616832 | tf_op jit(solution)/shard_map/all_gather | solution.py:33
  254.9 90.0 %copy-start.38 = (bf16[3]{0:T(256)(128)(2,1)S(1)}, bf16[3]{0:T(256)(128)(2,1)}, u32[]{:S(2)}) copy-start(bf16[3]{0:T(256)(128)(2,1)} %param.18) | copy-start | bytes 22
  254.9 196.1 %copy-start.36 = (bf16[6]{0:T(256)(128)(2,1)S(1)}, bf16[6]{0:T(256)(128)(2,1)}, u32[]{:S(2)}) copy-start(bf16[6]{0:T(256)(128)(2,1)} %param.19) | copy-start | bytes 40
  254.9 196.2 %copy-start.35 = (bf16[6,16]{1,0:T(8,128)(2,1)S(1)}, bf16[6,16]{1,0:T(8,128)(2,1)}, u32[]{:S(2)}) copy-start(bf16[6,16]{1,0:T(8,128)(2,1)} %param.20) | copy-start | bytes 580
  631.6 195.8 %copy-start.19 = (f32[768]{0:T(1024)}, f32[768]{0:T(1024)S(1)}, u32[]{:S(2)}) copy-start(f32[768]{0:T(1024)S(1)} %convert_reduce_fusion) | copy-start | bytes 9220
  719.5 107.9 %copy-start.2 = (f32[256,768]{1,0:T(8,128)}, f32[256,768]{1,0:T(8,128)S(1)}, u32[]{:S(2)}) copy-start(f32[256,768]{1,0:T(8,128)S(1)} %get-tuple-element.30) | copy-start | bytes 2359300
  719.5 107.8 %copy-start.24 = (f32[256]{0:T(256)}, f32[256]{0:T(256)S(1)}, u32[]{:S(2)}) copy-start(f32[256]{0:T(256)S(1)} %add_rsqrt_fusion) | copy-start | bytes 3076
  721.1 21.6 %all-to-all-start = ((bf16[16,40,768]{2,1,0:T(8,128)(2,1)}), bf16[16,40,768]{2,1,0:T(8,128)(2,1)}, u32[]{:S(2)}, u32[]{:S(2)}) async-start(bf16[16,40,768]{2,1,0:T(8,128)(2,1)} %bitcast.15), calls=%async_computation | async-start | bytes 1966080 | tf_op jit(solution)/shard_map/all_to_all | solution.py:185
  742.7 33.4 %all-to-all-start.2 = ((bf16[16,40,768]{2,1,0:T(8,128)(2,1)}), bf16[16,40,768]{2,1,0:T(8,128)(2,1)}, u32[]{:S(2)}, u32[]{:S(2)}) async-start(bf16[16,40,768]{2,1,0:T(8,128)(2,1)} %bitcast.236), calls=%async_computation.2 | async-start | bytes 1966080 | tf_op jit(solution)/shard_map/all_to_all | solution.py:215
  776.1 24.6 %all-to-all-start.1 = ((bf16[16,40,768]{2,1,0:T(8,128)(2,1)}), bf16[16,40,768]{2,1,0:T(8,128)(2,1)S(1)}, u32[]{:S(2)}, u32[]{:S(2)}) async-start(bf16[16,40,768]{2,1,0:T(8,128)(2,1)} %bitcast.237), calls=%async_computation.1 | async-start | bytes 1966080 | tf_op jit(solution)/shard_map/all_to_all | solution.py:196
  801.7 23.9 %all-to-all-start.3 = ((bf16[16,40,768]{2,1,0:T(8,128)(2,1)}), bf16[16,40,768]{2,1,0:T(8,128)(2,1)S(1)}, u32[]{:S(2)}, u32[]{:S(2)}) async-start(bf16[16,40,768]{2,1,0:T(8,128)(2,1)} %bitcast.234), calls=%async_computation.3 | async-start | bytes 1966080 | tf_op jit(solution)/shard_map/all_to_all | solution.py:240
  808.2 154.1 %reduce-scatter.25.cloned.1.call-start = ((), (), s32[]{:S(2)}) async-start(), calls=%async_computation.15 | async-start | bytes 7077888 | tf_op jit(solution)/shard_map/reduce_scatter | solution.py:285
  895.1 165.6 %reduce-scatter.29.cloned.1.call-start = ((), (), s32[]{:S(2)}) async-start(), calls=%async_computation.17 | async-start | bytes 3538944 | tf_op jit(solution)/shard_map/reduce_scatter | solution.py:54
  899.9 160.9 %reduce-scatter.27.cloned.1.call-start = ((), (), s32[]{:S(2)}) async-start(), calls=%async_computation.16 | async-start | bytes 10616832 | tf_op jit(solution)/shard_map/reduce_scatter | solution.py:54
  908.4 57.7 %copy-start.7 = (f32[1,256,768]{2,1,0:T(8,128)S(1)}, f32[1,256,768]{2,1,0:T(8,128)}, u32[]{:S(2)}) copy-start(f32[1,256,768]{2,1,0:T(8,128)} %param.12) | copy-start | bytes 2359300
  908.4 57.7 %copy-start.22 = (f32[768]{0:T(1024)S(1)}, f32[768]{0:T(1024)}, u32[]{:S(2)}) copy-start(f32[768]{0:T(1024)} %copy-done.21) | copy-start | bytes 9220
  908.5 57.7 %copy-start.29 = (f32[256]{0:T(256)S(1)}, f32[256]{0:T(256)}, u32[]{:S(2)}) copy-start(f32[256]{0:T(256)} %copy-done.28) | copy-start | bytes 3076
  973.3 88.7 %reduce-scatter.35.cloned.1.call-start = ((), (), s32[]{:S(2)}) async-start(), calls=%async_computation.21 | async-start | bytes 98304
  1012.2 50.6 %reduce-scatter.37.cloned.1.call-start = ((), (), s32[]{:S(2)}) async-start(), calls=%async_computation.22 | async-start | bytes 98304
  1013.6 50.0 %reduce-scatter.39.cloned.1.call-start = ((), (), s32[]{:S(2)}) async-start(), calls=%async_computation.23 | async-start | bytes 98304
  1015.6 95.7 %reduce-scatter.41.cloned.1.call-start = ((), (), s32[]{:S(2)}) async-start(), calls=%async_computation.24 | async-start | bytes 5308416
  1051.3 119.3 %reduce-scatter.31.cloned.1.call-start = ((), (), s32[]{:S(2)}) async-start(), calls=%async_computation.18 | async-start | bytes 5308416 | tf_op jit(solution)/shard_map/reduce_scatter | solution.py:236
  1059.7 113.6 %copy-start.9 = (f32[256,768]{1,0:T(8,128)S(1)}, f32[256,768]{1,0:T(8,128)}, u32[]{:S(2)}) copy-start(f32[256,768]{1,0:T(8,128)} %copy-done.8) | copy-start | bytes 2359300
  1059.7 113.6 %copy-start.23 = (f32[768]{0:T(1024)S(1)}, f32[768]{0:T(1024)}, u32[]{:S(2)}) copy-start(f32[768]{0:T(1024)} %copy-done.21) | copy-start | bytes 9220
  1059.7 113.6 %copy-start.30 = (f32[256]{0:T(256)S(1)}, f32[256]{0:T(256)}, u32[]{:S(2)}) copy-start(f32[256]{0:T(256)} %copy-done.28) | copy-start | bytes 3076
  1059.8 122.4 %reduce-scatter.33.cloned.1.call-start = ((), (), s32[]{:S(2)}) async-start(), calls=%async_computation.20 | async-start | bytes 98304
  1060.6 479.2 %all-reduce.11.cloned.1.call-start = ((), (), s32[]{:S(2)}) async-start(), calls=%async_computation.25 | async-start | bytes 9437184
  (28 other events, 311.8 us)
Sparse Core Ops, SparseCore 0:
  10.3 204.1 all-gather.9
  231.8 70.5 all-gather.5
  304.6 101.2 all-gather.7
  895.3 67.0 reduce-scatter.24
  964.6 11.3 reduce-scatter.28
  978.3 19.4 reduce-scatter.26
  1012.4 8.8 reduce-scatter.34
  1024.2 11.4 reduce-scatter.36
  1038.0 11.4 reduce-scatter.38
  1051.7 59.4 reduce-scatter.40
  1113.7 56.8 reduce-scatter.30
  1173.3 8.7 reduce-scatter.32
  1187.1 143.9 all-reduce.10
where the time goes:
time: 1560 us; the launch traced here: 1550 us
  blocking collectives  633 us (41%)
  waiting for transfers between devices  392 us (25%)
  local copies, waits for them, and re-layouts  224 us (14%)
  matrix products  197 us (13%)
  other arithmetic  65.9 us (4%)
  starting transfers between devices  24.1 us (2%)
    unnamed x2, blocking collectives  459 us
    all_gather x1, waiting for transfers between devices, side_by_side(): filled, at, done = (lax.all_gather(both, axis, axis=dim, tiled=True), 0, [])  204 us
    all_gather x1, blocking collectives, side_by_side(): filled, at, done = (lax.all_gather(both, axis, axis=dim, tiled=True), 0, [])  174 us
    and x1, local copies, waits for them, and re-layouts, shards(): (clipped[None] >= bucket_starts[:, None, None]) & (clipped[None] < bucket...  89.9 us
    unnamed x108, local copies, waits for them, and re-layouts  63.3 us
    unnamed x19, waiting for transfers between devices  54.5 us
    reduce_scatter x1, waiting for transfers between devices, shards(): lax.psum_scatter(kv_terms.astype(jnp.bfloat16), SEQ, scatter_dimension=1,...  53.5 us
    reduce_scatter x1, waiting for transfers between devices, shards(): lax.psum_scatter(grad_weight_out[None].astype(jnp.bfloat16), SEQ, scatter...  52.5 us
  transfers between devices with their start and end apart: 17, of which 8 were waited for; matrix products, arithmetic and copies ran while one was open for 25% of the time, Pallas kernels for 0%

commit v1 on v0

v1 whole, which is shorter than its diff:
```python
import math

import jax
import jax.numpy as jnp
from jax import lax
from jax.experimental import pallas as pl
from jax.experimental.pallas import tpu as pltpu
from jax.sharding import Mesh
from jax.sharding import PartitionSpec as P

D = 768
HEADS = 12
HEAD_DIM = 64
BUCKETS = 32
DP = ("dp_0", "dp_1", "dp_2")
SEQ = ("seq_0", "seq_1")
SEQ_DP = SEQ + DP
N_SEQ = 8
N_DP = 16
N_ALL = N_SEQ * N_DP
SHARD = D // N_ALL
ROWS = 256
LENGTH = N_SEQ * ROWS
TILES = LENGTH // ROWS
CHUNK = 2 * ROWS
PAIR = 2 * HEAD_DIM
GROUP = 3 * PAIR
MASKED = -1e30
VMEM_LIMIT = 56 * 1024 * 1024
NT = (((1,), (1,)), ((), ()))
F32 = jnp.float32
BF16 = jnp.bfloat16


def exchange(value, axes):
    return lax.all_to_all(value, axes, split_axis=0, concat_axis=0, tiled=True)


def after(value, earlier):
    return lax.optimization_barrier((value, earlier))[0]


def normalize(values):
    multiplier = lax.rsqrt(jnp.mean(values * values, axis=-1, keepdims=True) + 1e-06)
    return (values * multiplier, multiplier)


def norm_back(grad_normed, normed, multiplier):
    return multiplier * (
        grad_normed - normed * jnp.mean(grad_normed * normed, axis=-1, keepdims=True)
    )


def two_parts(value):
    high = lax.reduce_precision(value, 8, 7)
    return high.astype(BF16), (value - high).astype(BF16)


def fill_tiles(bias_ref, tiles_ref):
    for h in range(2):
        for b in range(TILES):
            low = LENGTH - ROWS * b
            row = jnp.concatenate(
                [bias_ref[h : h + 1, low : low + ROWS], bias_ref[h : h + 1, low - ROWS : low]], axis=1
            )
            turned = pltpu.roll(
                jnp.broadcast_to(row, (ROWS, 2 * ROWS)), 0, 1, stride=1, stride_axis=0
            )
            tiles_ref[h, ROWS * b : ROWS * (b + 1), :] = turned[:, :ROWS]
        tiles_ref[h, LENGTH:, :] = jnp.full((ROWS, ROWS), MASKED, F32)


def work_item(items_ref, n):
    block = items_ref[n]
    head = (n >= TILES).astype(jnp.int32)
    start = pl.multiple_of(block * ROWS, ROWS)
    offset = (TILES - 1 - block) * ROWS
    chunks = (block + 2) // 2
    mine = lax.broadcasted_iota(jnp.int32, (ROWS, PAIR), 1) // HEAD_DIM == head
    return block, head, start, offset, chunks, mine


def forward_kernel(items_ref, bias_ref, qkv_ref, out_ref, lse_ref, tiles_ref, vt_ref, s_ref):
    fill_tiles(bias_ref, tiles_ref)
    vt_ref[...] = qkv_ref[:, 2 * PAIR :].T
    out_ref[...] = jnp.zeros_like(out_ref)

    def item(n, carry):
        block, head, start, offset, chunks, mine = work_item(items_ref, n)
        q = qkv_ref[pl.ds(start, ROWS), :PAIR]
        q = jnp.where(mine, q.astype(F32) * (1.0 / math.sqrt(HEAD_DIM)), 0.0).astype(BF16)

        def score(c, top):
            at = pl.multiple_of(c * CHUNK, CHUNK)
            k = qkv_ref[pl.ds(at, CHUNK), PAIR : 2 * PAIR]
            s = lax.dot_general(k, q, NT, preferred_element_type=F32)
            s = s + tiles_ref[head, pl.ds(pl.multiple_of(offset + at, ROWS), CHUNK), :]
            s_ref[pl.ds(at, CHUNK), :] = s
            return jnp.maximum(top, jnp.max(s, axis=0, keepdims=True))

        top = lax.fori_loop(0, chunks, score, jnp.full((1, ROWS), MASKED, F32))

        def mix(c, sums):
            total, acc = sums
            at = pl.multiple_of(c * CHUNK, CHUNK)
            p = jnp.exp(s_ref[pl.ds(at, CHUNK), :] - top)
            acc = acc + jnp.dot(
                vt_ref[:, pl.ds(at, CHUNK)], p.astype(BF16), preferred_element_type=F32
            )
            return total + jnp.sum(p, axis=0, keepdims=True), acc

        total, acc = lax.fori_loop(
            0, chunks, mix, (jnp.zeros((1, ROWS), F32), jnp.zeros((PAIR, ROWS), F32))
        )
        lse_ref[head, block] = top + jnp.log(total)
        old = out_ref[pl.ds(start, ROWS), :].astype(F32)
        out_ref[pl.ds(start, ROWS), :] = jnp.where(mine, (acc / total).T, old).astype(BF16)
        return carry

    lax.fori_loop(0, TILES + TILES // 2, item, 0)


def backward_kernel(
    items_ref, bias_ref, qkv_ref, grad_ref, lse_ref, dqkv_ref, dbias_ref,
    tiles_ref, kt_ref, p_ref, dp_ref, dtiles_ref, dk_ref, dv_ref,
):
    fill_tiles(bias_ref, tiles_ref)
    kt_ref[...] = qkv_ref[:, PAIR : 2 * PAIR].T
    dtiles_ref[...] = jnp.zeros_like(dtiles_ref)
    dk_ref[...] = jnp.zeros_like(dk_ref)
    dv_ref[...] = jnp.zeros_like(dv_ref)
    dqkv_ref[:, :PAIR] = jnp.zeros((LENGTH, PAIR), BF16)
    dbias_ref[...] = jnp.zeros_like(dbias_ref)
    scale = 1.0 / math.sqrt(HEAD_DIM)

    def item(n, carry):
        block, head, start, offset, chunks, mine = work_item(items_ref, n)
        q = qkv_ref[pl.ds(start, ROWS), :PAIR]
        q = jnp.where(mine, q.astype(F32) * scale, 0.0).astype(BF16)
        g = jnp.where(mine, grad_ref[pl.ds(start, ROWS), :].astype(F32), 0.0).astype(BF16)
        lse = lse_ref[head, block]

        def first(c, inner):
            at = pl.multiple_of(c * CHUNK, CHUNK)
            k = qkv_ref[pl.ds(at, CHUNK), PAIR : 2 * PAIR]
            v = qkv_ref[pl.ds(at, CHUNK), 2 * PAIR :]
            s = lax.dot_general(k, q, NT, preferred_element_type=F32)
            s = s + tiles_ref[head, pl.ds(pl.multiple_of(offset + at, ROWS), CHUNK), :]
            p = jnp.exp(s - lse)
            dp = lax.dot_general(v, g, NT, preferred_element_type=F32)
            p_ref[pl.ds(at, CHUNK), :] = p
            dp_ref[pl.ds(at, CHUNK), :] = dp
            return inner + jnp.sum(p * dp, axis=0, keepdims=True)

        inner = lax.fori_loop(0, chunks, first, jnp.zeros((1, ROWS), F32))

        def second(c, dq):
            at = pl.multiple_of(c * CHUNK, CHUNK)
            p = p_ref[pl.ds(at, CHUNK), :]
            ds = p * (dp_ref[pl.ds(at, CHUNK), :] - inner)
            there = pl.ds(pl.multiple_of(offset + at, ROWS), CHUNK)
            dtiles_ref[head, there, :] = dtiles_ref[head, there, :] + ds
            ds = ds.astype(BF16)
            here = pl.ds(at, CHUNK)
            dk_ref[here, :] = dk_ref[here, :] + jnp.dot(ds, q, preferred_element_type=F32)
            dv_ref[here, :] = dv_ref[here, :] + jnp.dot(
                p.astype(BF16), g, preferred_element_type=F32
            )
            return dq + jnp.dot(kt_ref[:, here], ds, preferred_element_type=F32)

        dq = lax.fori_loop(0, chunks, second, jnp.zeros((PAIR, ROWS), F32))
        old = dqkv_ref[pl.ds(start, ROWS), :PAIR].astype(F32)
        dqkv_ref[pl.ds(start, ROWS), :PAIR] = jnp.where(mine, (dq * scale).T, old).astype(BF16)
        return carry

    lax.fori_loop(0, TILES + TILES // 2, item, 0)
    dqkv_ref[:, PAIR : 2 * PAIR] = dk_ref[...].astype(BF16)
    dqkv_ref[:, 2 * PAIR :] = dv_ref[...].astype(BF16)
    row_of = lax.broadcasted_iota(jnp.int32, (8, 2 * ROWS), 0)
    for h in range(2):
        for b in range(TILES):
            part = dtiles_ref[h, ROWS * b : ROWS * (b + 1), :]
            part = jnp.concatenate([part, jnp.zeros_like(part)], axis=1)
            half = ROWS // 2
            while half >= 8:
                part = part[:half] + pltpu.roll(part[half:], 2 * ROWS - half, 1)
                half //= 2
            for bit in (4, 2, 1):
                part = jnp.where(
                    (row_of & bit) != 0, pltpu.roll(part, 2 * ROWS - bit, 1), part
                )
            line = jnp.sum(part, axis=0, keepdims=True)
            low = LENGTH - ROWS * b
            dbias_ref[h : h + 1, low : low + ROWS] += line[:, :ROWS]
            dbias_ref[h : h + 1, low - ROWS : low] += line[:, ROWS:]


def in_vmem(count):
    return [pl.BlockSpec(memory_space=pltpu.VMEM)] * count


def attention_forward(items, bias, qkv):
    return pl.pallas_call(
        forward_kernel,
        out_shape=(
            jax.ShapeDtypeStruct((LENGTH, PAIR), BF16),
            jax.ShapeDtypeStruct((2, TILES, 1, ROWS), F32),
        ),
        in_specs=[pl.BlockSpec(memory_space=pltpu.SMEM)] + in_vmem(2),
        out_specs=tuple(in_vmem(2)),
        scratch_shapes=[
            pltpu.VMEM((2, LENGTH + ROWS, ROWS), F32),
            pltpu.VMEM((PAIR, LENGTH), BF16),
            pltpu.VMEM((LENGTH, ROWS), F32),
        ],
        compiler_params=pltpu.CompilerParams(vmem_limit_bytes=VMEM_LIMIT),
        name="attention_forward",
    )(items, bias, qkv)


def attention_backward(items, bias, qkv, grad, lse):
    return pl.pallas_call(
        backward_kernel,
        out_shape=(
            jax.ShapeDtypeStruct((LENGTH, GROUP), BF16),
            jax.ShapeDtypeStruct((8, LENGTH + ROWS), F32),
        ),
        in_specs=[pl.BlockSpec(memory_space=pltpu.SMEM)] + in_vmem(4),
        out_specs=tuple(in_vmem(2)),
        scratch_shapes=[
            pltpu.VMEM((2, LENGTH + ROWS, ROWS), F32),
            pltpu.VMEM((PAIR, LENGTH), BF16),
            pltpu.VMEM((LENGTH, ROWS), F32),
            pltpu.VMEM((LENGTH, ROWS), F32),
            pltpu.VMEM((2, LENGTH + ROWS, ROWS), F32),
            pltpu.VMEM((LENGTH, PAIR), F32),
            pltpu.VMEM((LENGTH, PAIR), F32),
        ],
        compiler_params=pltpu.CompilerParams(vmem_limit_bytes=VMEM_LIMIT),
        name="attention_backward",
    )(items, bias, qkv, grad, lse)


ERFC = (
    0.22562630138780296, 0.22657565341666724, 0.2009589960079044, 0.19696137866341243, 0.07151224844545567,
    0.09972378565249672, 0.07384727982904729, -0.13547360506233205, 0.040268019240819755,
)


def gelu_and_slope(values):
    size = jnp.abs(values)
    base = 1.0 + (0.4 * 0.7071067811865476) * size
    t = pl.reciprocal(base, approx=True)
    t = t * (2.0 - base * t)
    tail = jnp.full_like(values, 0.5 * ERFC[-1])
    for factor in ERFC[-2::-1]:
        tail = tail * t + 0.5 * factor
    bell = jnp.exp2((-0.5 / math.log(2.0)) * values * values)
    tail = tail * t * bell
    share = jnp.where(values >= 0.0, 1.0 - tail, tail)
    return values * share, share + values * bell * 0.3989422804014327


def expert_forward_kernel(arrived_ref, weight_ref, act_ref, slope_ref, produced_ref, total_ref):
    c = pl.program_id(0)

    @pl.when(c == 0)
    def _():
        total_ref[...] = jnp.zeros_like(total_ref)

    preact = lax.dot_general(
        arrived_ref[...], weight_ref[:, :D], NT, preferred_element_type=F32
    )
    act, slope = gelu_and_slope(preact)
    act = act.astype(BF16)
    act_ref[...] = act
    slope_ref[...] = slope
    total_ref[...] += jnp.dot(act, weight_ref[:, D:], preferred_element_type=F32)

    @pl.when(c == pl.num_programs(0) - 1)
    def _():
        produced_ref[...] = total_ref[...].astype(BF16)


def expert_forward(arrived, weight):
    rows, hidden = arrived.shape[0], weight.shape[0]
    block = hidden // 12
    return pl.pallas_call(
        expert_forward_kernel,
        grid=(hidden // block,),
        out_shape=(
            jax.ShapeDtypeStruct((rows, hidden), BF16),
            jax.ShapeDtypeStruct((rows, hidden), F32),
            jax.ShapeDtypeStruct((rows, D), BF16),
        ),
        in_specs=[
            pl.BlockSpec((rows, D), lambda c: (0, 0)),
            pl.BlockSpec((block, 2 * D), lambda c: (c, 0)),
        ],
        out_specs=(
            pl.BlockSpec((rows, block), lambda c: (0, c)),
            pl.BlockSpec((rows, block), lambda c: (0, c)),
            pl.BlockSpec((rows, D), lambda c: (0, 0)),
        ),
        scratch_shapes=[pltpu.VMEM((rows, D), F32)],
        compiler_params=pltpu.CompilerParams(vmem_limit_bytes=VMEM_LIMIT),
        name="expert_forward",
    )(arrived, weight)


def expert_backward_kernel(incoming_ref, weight_ref, slope_ref, produced_ref, grad_ref, back_ref, total_ref):
    c = pl.program_id(0)

    @pl.when(c == 0)
    def _():
        total_ref[...] = jnp.zeros_like(total_ref)
        back_ref[:, :D] = produced_ref[...]

    grad_act = lax.dot_general(
        incoming_ref[...], weight_ref[:, D:], NT, preferred_element_type=F32
    )
    grad = (grad_act * slope_ref[...]).astype(BF16)
    grad_ref[...] = grad
    total_ref[...] += jnp.dot(grad, weight_ref[:, :D], preferred_element_type=F32)

    @pl.when(c == pl.num_programs(0) - 1)
    def _():
        back_ref[:, D:] = total_ref[...].astype(BF16)


def expert_backward(incoming, weight, slope, produced):
    rows, hidden = slope.shape
    block = hidden // 6
    whole = pl.BlockSpec((rows, D), lambda c: (0, 0))
    return pl.pallas_call(
        expert_backward_kernel,
        grid=(hidden // block,),
        out_shape=(
            jax.ShapeDtypeStruct((rows, hidden), BF16),
            jax.ShapeDtypeStruct((rows, 2 * D), BF16),
        ),
        in_specs=[
            whole,
            pl.BlockSpec((block, 2 * D), lambda c: (c, 0)),
            pl.BlockSpec((rows, block), lambda c: (0, c)),
            whole,
        ],
        out_specs=(
            pl.BlockSpec((rows, block), lambda c: (0, c)),
            pl.BlockSpec((rows, 2 * D), lambda c: (0, 0)),
        ),
        scratch_shapes=[pltpu.VMEM((rows, D), F32)],
        compiler_params=pltpu.CompilerParams(vmem_limit_bytes=VMEM_LIMIT),
        name="expert_backward",
    )(incoming, weight, slope, produced)


def weight_grad_kernel(hidden_ref, rows_ref, grad_ref):
    grad_ref[...] = lax.dot_general(
        hidden_ref[...], rows_ref[...], (((0,), (0,)), ((), ())), preferred_element_type=F32
    ).astype(BF16)


def weight_grad(hidden_rows, rows, name):
    count, hidden = hidden_rows.shape
    block = hidden // 4
    return pl.pallas_call(
        weight_grad_kernel,
        grid=(hidden // block,),
        in_specs=[
            pl.BlockSpec((count, block), lambda c: (0, c)),
            pl.BlockSpec((count, D), lambda c: (0, 0)),
        ],
        out_specs=pl.BlockSpec((block, D), lambda c: (c, 0)),
        out_shape=jax.ShapeDtypeStruct((hidden, D), BF16),
        compiler_params=pltpu.CompilerParams(vmem_limit_bytes=VMEM_LIMIT),
        name=name,
    )(hidden_rows, rows)


def input_grad_kernel(places_ref, rows_ref, weight_ref, middle_ref, normed_ref, factor_ref, gain_ref, out_ref):
    total = jnp.zeros((ROWS, D), F32)
    for c in range(N_SEQ):
        total += lax.dot_general(
            rows_ref[places_ref[c]], weight_ref[c], NT, preferred_element_type=F32
        )
    grad = total * gain_ref[...]
    out_ref[...] = middle_ref[...] + norm_back(grad, normed_ref[...], factor_ref[...])


def input_gradient(places, rows, weight, grad_middle, normed, factor, gain):
    return pl.pallas_call(
        input_grad_kernel,
        out_shape=jax.ShapeDtypeStruct((ROWS, D), F32),
        in_specs=[pl.BlockSpec(memory_space=pltpu.SMEM)] + in_vmem(6),
        out_specs=pl.BlockSpec(memory_space=pltpu.VMEM),
        compiler_params=pltpu.CompilerParams(vmem_limit_bytes=VMEM_LIMIT),
        name="input_gradient",
    )(places, rows, weight, grad_middle, normed, factor, gain)


def pass_y(value):
    return lax.ppermute(value, SEQ[0], [(0, 1), (1, 0)])


def gather_x(block, other, ready):
    both = jnp.concatenate([block, other])
    both = both if ready is None else after(both, ready)
    return lax.all_gather(both, SEQ[1], axis=0, tiled=True)


def scatter_x(value):
    return lax.psum_scatter(value, SEQ[1], scatter_dimension=0, tiled=True)


def sum_y(part):
    half = part.shape[0] // 2
    other = pass_y(part[half:])
    return part[:half].astype(F32) + other.astype(F32), other


def gather_dp(block):
    return exchange(jnp.broadcast_to(block, (N_DP, *block.shape)), DP)


def in_order(gathered):
    width = gathered.shape[-1]
    gathered = gathered.reshape(N_DP, N_SEQ, SHARD, width)
    return gathered.transpose(1, 0, 2, 3).reshape(D, width)


def shards(
    inputs,
    routes,
    buckets,
    norm1_gain,
    qkv_weight,
    out_weight,
    rel_bias,
    norm2_gain,
    router_projection_weight,
    expert_in,
    expert_out,
    cotangent,
):
    seq_index = lax.axis_index(SEQ)
    capacity = 10 * ROWS // (4 * N_DP)
    routed_rows = N_DP * capacity

    flat_in = inputs.reshape(ROWS, D)
    normed_one, factor_one = normalize(flat_in)
    normed = normed_one.astype(BF16)
    normed_other = pass_y(normed)

    parts = qkv_weight.reshape(SHARD, 3, 4, 3, HEAD_DIM)
    parts = jnp.concatenate([parts[:, :, :, c] for c in (0, 1, 2, 1)], axis=-1)
    parts = parts.reshape(SHARD, 3, N_SEQ, PAIR).transpose(2, 0, 1, 3).reshape(N_SEQ, SHARD, GROUP)
    extra = jnp.stack([norm1_gain, jnp.pad(rel_bias, (0, SHARD - rel_bias.shape[0]))], axis=1)
    extra = jnp.pad(extra, ((0, 0), (0, 126)))
    parts = jnp.concatenate([parts, jnp.broadcast_to(extra, (N_SEQ, SHARD, 128))], axis=-1)
    second = [out_weight, router_projection_weight, norm2_gain[:, None]]
    parts = [parts] + [jnp.broadcast_to(p, (N_SEQ, SHARD, p.shape[-1])) for p in second]
    parts = jnp.concatenate(parts, axis=-1)
    parts = jnp.pad(parts, ((0, 0), (0, 0), (0, -parts.shape[-1] % 128)))
    parts = exchange(parts, SEQ).reshape(N_SEQ * SHARD, parts.shape[-1])
    normed_other = after(normed_other, parts)
    is_low = lax.axis_index(SEQ[0]) == 0
    normed = jnp.stack(
        [jnp.where(is_low, normed, normed_other), jnp.where(is_low, normed_other, normed)]
    )
    normed_all = lax.all_gather(normed, SEQ[1])
    first = gather_dp(parts[:, : GROUP + 128])
    second = gather_dp(after(parts[:, GROUP + 128 :], first))

    expert_rows = jnp.concatenate([expert_in[0].T, expert_out[0]], axis=1)
    expert_full = gather_x(expert_rows, pass_y(expert_rows), (first, normed_all))
    first = in_order(first)
    normed_all = after(normed_all, first).transpose(1, 0, 2, 3).reshape(LENGTH, D)
    pair_weight = first[:, :GROUP]
    gain_one = first[:, GROUP].astype(F32)
    bias_table = first[:, GROUP + 1].reshape(N_ALL, SHARD)[:, : rel_bias.shape[0]]
    bias_table = bias_table.reshape(HEADS, BUCKETS)

    route_pairs = routes.reshape(ROWS, 2).T
    expert_range = jnp.arange(N_DP, dtype=jnp.int32)
    onehot = (route_pairs[:, :, None] == expert_range[None, None, :]).astype(F32)
    named = onehot[0] + onehot[1]
    earlier = (
        jnp.arange(ROWS, dtype=jnp.int32)[:, None] > jnp.arange(ROWS, dtype=jnp.int32)[None, :]
    ).astype(BF16)
    before = jnp.dot(earlier, named.astype(BF16), preferred_element_type=F32)
    slot = jnp.sum(onehot * before[None], axis=-1).astype(jnp.int32)
    target = (route_pairs * capacity + slot).reshape(2 * ROWS)
    slots = jnp.arange(routed_rows, dtype=jnp.int32)
    take_map = (target[:, None] == slots[None, :]).astype(BF16)
    send_map = (slots[:, None] == target[None, :]).astype(BF16)
    token_send = send_map[:, :ROWS] + send_map[:, ROWS:]
    token_take = take_map[:ROWS] + take_map[ROWS:]

    h_one = (normed_all.astype(F32) * gain_one).astype(BF16)
    qkv = jnp.dot(h_one, pair_weight, preferred_element_type=F32).astype(BF16)
    reach = jnp.concatenate([jnp.full((ROWS,), -1, jnp.int32), buckets])
    reach_onehot = reach[None, :] == jnp.arange(BUCKETS, dtype=jnp.int32)[:, None]
    group = seq_index // 2
    parity = seq_index % 2
    own = jnp.stack([3 * group + 2 * parity, 3 * group + 1])
    own_onehot = jnp.arange(HEADS, dtype=jnp.int32)[None, :] == own[:, None]
    own_bias = jnp.sum(
        jnp.where(own_onehot[:, :, None], bias_table.astype(F32)[None], 0.0), axis=1
    )
    distance_bias = jnp.sum(
        jnp.where(reach_onehot[None], own_bias[:, :, None], 0.0), axis=1
    )
    distance_bias = jnp.where(reach[None, :] < 0, MASKED, distance_bias)
    distance_bias = jnp.pad(distance_bias, ((0, 6), (0, 0)))
    shared_blocks = jnp.where(
        parity == 0, jnp.array([0, 3, 4, 7], jnp.int32), jnp.array([1, 2, 5, 6], jnp.int32)
    )
    items = jnp.concatenate([jnp.arange(TILES, dtype=jnp.int32), shared_blocks])
    attended_pair, lse = attention_forward(items, distance_bias, qkv)
    pair_other = pass_y(pair_weight)
    attended_pair, pair_other, second = lax.optimization_barrier(
        (attended_pair, pair_other, second)
    )
    second = in_order(second)
    out_full = second[:, :D].reshape(4, 3, HEAD_DIM, D)
    out_pairs = jnp.concatenate([out_full[:, c] for c in (0, 1, 2, 1)], axis=1).reshape(
        N_SEQ * PAIR, D
    )
    router_full = second[:, D : D + N_DP]
    gain_two = second[:, D + N_DP].astype(F32)
    attended = exchange(attended_pair.reshape(N_SEQ, ROWS, PAIR), SEQ)
    attended = attended.transpose(1, 0, 2).reshape(ROWS, N_SEQ * PAIR)
    middle = flat_in + jnp.dot(attended, out_pairs, preferred_element_type=F32)

    normed_two, factor_two = normalize(middle)
    h_two = (normed_two * gain_two).astype(BF16)
    outgoing = jnp.dot(token_send, h_two, preferred_element_type=F32).astype(BF16)
    arrived = exchange(outgoing.reshape(N_DP, capacity, D), DP).reshape(routed_rows, D)

    logits = jnp.dot(h_two, router_full, preferred_element_type=F32)
    chosen = jnp.sum(logits[None] * onehot, axis=-1)
    gates = jax.nn.softmax(chosen, axis=0)
    grad_out = cotangent.reshape(ROWS, D)
    grad_assign = (gates[:, :, None] * grad_out[None]).astype(BF16).reshape(2 * ROWS, D)
    outgoing_grad = jnp.dot(send_map, grad_assign, preferred_element_type=F32).astype(BF16)
    incoming = exchange(outgoing_grad.reshape(N_DP, capacity, D), DP).reshape(routed_rows, D)

    activated, slope, produced = expert_forward(arrived, expert_full)
    produced = after(produced, incoming)
    weight_pairs = gather_x(pair_weight, pair_other, arrived).reshape(N_SEQ, D, GROUP)
    grad_preact, back = expert_backward(incoming, expert_full, slope, produced)
    back = exchange(back.reshape(N_DP, capacity, 2 * D), DP).reshape(routed_rows, 2 * D)
    out_part = scatter_x(weight_grad(activated, incoming, "grad_expert_out"))
    out_shard, out_other = sum_y(out_part)
    in_part = scatter_x(
        after(weight_grad(grad_preact, arrived, "grad_expert_in"), weight_pairs)
    )
    returned, grad_back = back[:, :D], back[:, D:]

    picked = jnp.dot(take_map, returned, preferred_element_type=F32).reshape(2, ROWS, D)
    layer_out = middle + jnp.sum(gates[:, :, None] * picked, axis=0)
    grad_gates = jnp.sum(grad_out[None] * picked, axis=-1)
    grad_chosen = gates * (grad_gates - jnp.sum(gates * grad_gates, axis=0, keepdims=True))
    grad_logits = jnp.sum(grad_chosen[:, :, None] * onehot, axis=0)

    grad_h_two = jnp.dot(token_take, grad_back, preferred_element_type=F32)
    grad_h_two = grad_h_two + lax.dot_general(
        grad_logits, router_full.astype(F32), NT, precision=lax.Precision.HIGHEST
    )
    grad_router = jnp.dot(h_two.astype(F32).T, grad_logits, precision=lax.Precision.HIGHEST)
    grad_gain_two = jnp.sum(grad_h_two * normed_two, axis=0)
    grad_middle = grad_out + norm_back(grad_h_two * gain_two, normed_two, factor_two)
    grad_branch = grad_middle.astype(BF16)
    grad_attended = lax.dot_general(grad_branch, out_pairs, NT, preferred_element_type=F32)
    grad_attended = grad_attended.astype(BF16).reshape(ROWS, N_SEQ, PAIR).transpose(1, 0, 2)
    grad_pair = exchange(grad_attended, SEQ).reshape(LENGTH, PAIR)

    grad_out_pairs = jnp.einsum("tc,te->ce", attended, grad_branch, preferred_element_type=F32)
    grad_out_pairs = grad_out_pairs.reshape(4, 4, HEAD_DIM, D)
    grad_out_weight = jnp.stack(
        [grad_out_pairs[:, 0], grad_out_pairs[:, 1] + grad_out_pairs[:, 3], grad_out_pairs[:, 2]],
        axis=1,
    ).reshape(D, D)
    small = jnp.concatenate([grad_router, grad_gain_two[:, None]], axis=1)
    second_grads = jnp.concatenate([grad_out_weight.astype(BF16), *two_parts(small)], axis=1)
    second_grads = jnp.pad(second_grads, ((0, 0), (0, 7 * 128 - second_grads.shape[1])))
    second_grads = exchange(second_grads.reshape(N_ALL, SHARD, 7 * 128), SEQ_DP)
    second_sum = jnp.sum(second_grads.astype(F32), axis=0)
    out_grad = second_sum[:, :D]
    small_sum = second_sum[:, D : D + 17] + second_sum[:, D + 17 : D + 34]
    router_grad = small_sum[:, :N_DP]
    norm2_grad = small_sum[:, N_DP]

    grad_qkv, grad_reach = attention_backward(items, distance_bias, qkv, grad_pair, lse)
    grad_qkv = after(grad_qkv, (second_grads, out_other))
    grad_qkv_rows = exchange(grad_qkv.reshape(N_SEQ, ROWS, GROUP), SEQ)
    before_first = grad_qkv_rows
    in_shard, in_other = sum_y(after(in_part, grad_qkv_rows))
    in_shard = in_shard.T
    sources = jnp.arange(N_SEQ, dtype=jnp.int32)
    places = (sources % 2 ^ seq_index // 4) * 4 + sources // 2
    input_grad = input_gradient(
        places, grad_qkv_rows, weight_pairs, grad_middle, normed_one, factor_one, gain_one[None]
    )

    grad_pair_weight = jnp.einsum("td,te->de", h_one, grad_qkv, preferred_element_type=F32)
    grad_own_bias = jnp.sum(
        jnp.where(reach_onehot[None], grad_reach[:2, None, :], 0.0), axis=-1
    )
    grad_table = jnp.sum(
        jnp.where(own_onehot[:, :, None], grad_own_bias[:, None, :], 0.0), axis=0
    ).reshape(N_ALL, -1)
    grad_extra = jnp.stack(two_parts(grad_table), axis=-1)
    grad_extra = jnp.pad(grad_extra, ((0, 0), (0, SHARD - grad_extra.shape[1]), (0, 126)))
    first_grads = jnp.concatenate(
        [grad_pair_weight.astype(BF16).reshape(N_ALL, SHARD, GROUP), grad_extra], axis=-1
    )
    first_grads = exchange(after(first_grads, before_first), SEQ_DP)
    first_grads = after(first_grads, in_other).astype(F32)
    pair_sum = jnp.sum(first_grads.reshape(N_SEQ, N_DP, SHARD, GROUP + 128), axis=1)
    bias_sum = jnp.sum(pair_sum[:, : rel_bias.shape[0], GROUP : GROUP + 2], axis=(0, 2))
    pair_sum = pair_sum[:, :, :GROUP].reshape(4, 2, SHARD, 3, 2, HEAD_DIM)
    qkv_grad = jnp.stack(
        [pair_sum[:, 0, :, :, 0], pair_sum[:, 0, :, :, 1] + pair_sum[:, 1, :, :, 1], pair_sum[:, 1, :, :, 0]],
        axis=3,
    )
    qkv_grad = qkv_grad.transpose(1, 2, 0, 3, 4).reshape(SHARD, 3 * D)
    norm1_grad = jnp.sum(qkv_weight.astype(F32) * qkv_grad, axis=1) / norm1_gain.astype(F32)
    return (
        layer_out[None],
        input_grad[None],
        norm1_grad,
        qkv_grad,
        out_grad,
        bias_sum,
        norm2_grad,
        router_grad,
        in_shard[None],
        out_shard[None],
    )


def solution(mesh):
    torus = Mesh(mesh.devices.reshape(2, 4, 4, 2, 2), SEQ_DP)
    rows = P(DP, SEQ, None)
    spread = P(SEQ_DP)
    wide = P(SEQ_DP, None)
    in_specs = (
        rows,
        rows,
        P(),
        spread,
        wide,
        wide,
        spread,
        spread,
        wide,
        P(DP, None, SEQ),
        P(DP, SEQ, None),
        rows,
    )
    out_specs = (
        rows,
        rows,
        spread,
        wide,
        wide,
        spread,
        spread,
        wide,
        P(DP, None, SEQ),
        P(DP, SEQ, None),
    )
    return jax.shard_map(
        shards, mesh=torus, in_specs=in_specs, out_specs=out_specs, check_vma=False
    )
```

time: 1560 us -> 412 us (0.26)
  blocking collectives: 633 us -> 0 us
  waiting for transfers between devices: 392 us -> 131 us
  local copies, waits for them, and re-layouts: 224 us -> 29.9 us
  matrix products: 197 us -> 20.3 us
  Pallas kernels: 0 us -> 111 us
  starting transfers between devices: 24.1 us -> 73.1 us
  other arithmetic: 65.9 us -> 27.7 us
    unnamed x2 -> x0, blocking collectives: 459 us -> none
    all_gather x3, waiting for transfers between devices: 204 us -> 0.16 us  [the longest x1 0.14 us: shards(): normed_all = lax.all_gather(normed, SEQ[1])]
    dot_general x27 -> x13, matrix products: 197 us -> 20.3 us  [the longest x1 3.26 us: shards(): jnp.dot(take_map, returned, preferred_element_type=F32).reshape(2, ROWS, D)]
    all_gather x1 -> x0, blocking collectives: 174 us -> none  [side_by_side(): filled, at, done = (lax.all_gather(both, axis, axis=dim, tiled=True), 0, [])]
    pallas_call x0 -> x7, Pallas kernels: none -> 111 us  [the longest x1 31.2 us: attention_backward(): pl.pallas_call(backward_kernel, out_shape=(jax.ShapeDtypeStruct((LENGTH,...]
    reduce_scatter x4 -> x2, waiting for transfers between devices: 106 us -> 15.9 us  [scatter_x(): return lax.psum_scatter(value, SEQ[1], scatter_dimension=0, tiled=True)]
    and x1 -> x0, local copies, waits for them, and re-layouts: 89.9 us -> none  [shards(): (clipped[None] >= bucket_starts[:, None, None]) & (clipped[None] < bucket...]
    all_to_all x4 -> x11, waiting for transfers between devices: 27.8 us -> 95.3 us  [exchange(): return lax.all_to_all(value, axes, split_axis=0, concat_axis=0, tiled=True)]
  transfers between devices with their start and end apart: 17 -> 21, of which waited for: 8 -> 12; matrix products, arithmetic and copies ran while one was open for 25% -> 15% of each run, Pallas kernels for 0% -> 27%
where the time goes in v1:
time: 412 us; the launch traced here: 408 us
  waiting for transfers between devices  131 us (32%)
  Pallas kernels  111 us (27%)
  starting transfers between devices  73.1 us (18%)
  local copies, waits for them, and re-layouts  29.9 us (7%)
  other arithmetic  27.7 us (7%)
  matrix products  20.3 us (5%)
  between operations  14.8 us (4%)
    all_to_all x11, waiting for transfers between devices, exchange(): return lax.all_to_all(value, axes, split_axis=0, concat_axis=0, tiled=True)  95.3 us
    all_to_all x11, starting transfers between devices, exchange(): return lax.all_to_all(value, axes, split_axis=0, concat_axis=0, tiled=True)  68.3 us
    pallas_call x1, Pallas kernels, attention_backward(): pl.pallas_call(backward_kernel, out_shape=(jax.ShapeDtypeStruct((LENGTH,...  31.2 us
    pallas_call x1, Pallas kernels, expert_forward(): pl.pallas_call(expert_forward_kernel, grid=(hidden // block,), out_shape=...  24.9 us
    pallas_call x1, Pallas kernels, attention_forward(): pl.pallas_call(forward_kernel, out_shape=(jax.ShapeDtypeStruct((LENGTH, P...  19.6 us
    ppermute x5, waiting for transfers between devices, pass_y(): return lax.ppermute(value, SEQ[0], [(0, 1), (1, 0)])  19.5 us
    reduce_scatter x2, waiting for transfers between devices, scatter_x(): return lax.psum_scatter(value, SEQ[1], scatter_dimension=0, tiled=True)  15.9 us
    pallas_call x2, Pallas kernels, weight_grad(): pl.pallas_call(weight_grad_kernel, grid=(hidden // block,), in_specs=[pl....  15.3 us
  transfers between devices with their start and end apart: 21, of which 12 were waited for; matrix products, arithmetic and copies ran while one was open for 15% of the time, Pallas kernels for 27%

profile of v1, /device:TPU:0, one launch (start us, length us, event | category | flops | bytes accessed | tf_op | source)
XLA Modules:
  0.0 408.1 jit_solution(6098118931429910700)
XLA Ops:
  13.9 4.3 %all-to-all-start = ((bf16[8,6,1408]{2,1,0:T(8,128)(2,1)}), bf16[8,6,1408]{2,1,0:T(8,128)(2,1)S(1)}, u32[]{:S(2)}, u32[]{:S(2)}) async-start(bf16[8,6,1408]{2,1,0:T(8,128)(2,1)} %pad.27), calls=%async_computation | async-start | bytes 360448 | tf_op jit(solution)/shard_map/all_to_all | solution.py:36
  18.2 6.8 %all-to-all-done = bf16[8,6,1408]{2,1,0:T(8,128)(2,1)S(1)} async-done(((bf16[8,6,1408]{2,1,0:T(8,128)(2,1)}), bf16[8,6,1408]{2,1,0:T(8,128)(2,1)S(1)}, u32[]{:S(2)}, u32[]{:S(2)}) %all-to-all-start) | async-done | bytes 135200 | tf_op jit(solution)/shard_map/all_to_all | solution.py:36
  28.4 7.9 %all-to-all-start.1 = ((bf16[16,48,512]{2,1,0:T(8,128)(2,1)}), bf16[16,48,512]{2,1,0:T(8,128)(2,1)S(1)}, u32[]{:S(2)}, u32[]{:S(2)}) async-start(bf16[16,48,512]{2,1,0:T(8,128)(2,1)} %broadcast_in_dim.161), calls=%async_computation.1 | async-start | bytes 1572864 | tf_op jit(solution)/shard_map/all_to_all | solution.py:36
  36.4 19.5 %collective-permute-done.2 = bf16[384,1536]{1,0:T(8,128)(2,1)} collective-permute-done((bf16[384,1536]{1,0:T(8,128)(2,1)S(1)}, bf16[384,1536]{1,0:T(8,128)(2,1)}, u32[]{:S(2)}, u32[]{:S(2)}) %collective-permute-start.2) | collective-permute-done | bytes 1179680 | tf_op jit(solution)/shard_map/ppermute | solution.py:403
  55.9 2.8 pad_maximum_fusion
  58.7 7.9 %all-to-all-done.1 = bf16[16,48,512]{2,1,0:T(8,128)(2,1)S(1)} async-done(((bf16[16,48,512]{2,1,0:T(8,128)(2,1)}), bf16[16,48,512]{2,1,0:T(8,128)(2,1)S(1)}, u32[]{:S(2)}, u32[]{:S(2)}) %all-to-all-start.1) | async-done | bytes 786464 | tf_op jit(solution)/shard_map/all_to_all | solution.py:36
  70.8 7.0 %all-to-all-start.2 = ((bf16[16,48,896]{2,1,0:T(8,128)(2,1)}), bf16[16,48,896]{2,1,0:T(8,128)(2,1)S(1)}, u32[]{:S(2)}, u32[]{:S(2)}) async-start(bf16[16,48,896]{2,1,0:T(8,128)(2,1)} %broadcast_in_dim.166), calls=%async_computation.2 | async-start | bytes 2752512 | tf_op jit(solution)/shard_map/all_to_all | solution.py:36
  79.6 2.9 convert_bitcast_fusion
  85.1 3.0 convolution_convert_fusion.qkv_ref
  88.1 19.6 %attention_forward.1 = (bf16[2048,128]{1,0:T(8,128)(2,1)}, f32[2,8,1,256]{3,2,1,0:T(1,128)}) custom-call(s32[12]{0:T(128)} %pad_add_fusion.items_ref, f32[8,2304]{1,0:T(8,128)} %pad.28.bias_ref, bf16[2048,384]{1,0:T(8,128)(2,1)} %convolution_convert_fusion.qkv_ref), custom_call_target="tpu_custom_call" | custom-call | tf_op jit(solution)/shard_map/attention_forward/pallas_call | solution.py:203
  112.0 4.6 %all-to-all-start.3 = ((bf16[8,256,128]{1,2,0:T(8,128)(2,1)}), bf16[8,256,128]{1,2,0:T(8,128)(2,1)S(1)}, u32[]{:S(2)}, u32[]{:S(2)}) async-start(bf16[8,256,128]{1,2,0:T(8,128)(2,1)} %copy.207), calls=%async_computation.3 | async-start | bytes 1048576 | tf_op jit(solution)/shard_map/all_to_all | solution.py:36
  117.1 13.1 %all-to-all-done.3 = bf16[8,256,128]{1,2,0:T(8,128)(2,1)S(1)} async-done(((bf16[8,256,128]{1,2,0:T(8,128)(2,1)}), bf16[8,256,128]{1,2,0:T(8,128)(2,1)S(1)}, u32[]{:S(2)}, u32[]{:S(2)}) %all-to-all-start.3) | async-done | bytes 524320 | tf_op jit(solution)/shard_map/all_to_all | solution.py:36
  135.9 6.7 %all-to-all-start.5 = ((bf16[16,40,768]{2,1,0:T(8,128)(2,1)}), bf16[16,40,768]{2,1,0:T(8,128)(2,1)S(1)}, u32[]{:S(2)}, u32[]{:S(2)}) async-start(bf16[16,40,768]{2,1,0:T(8,128)(2,1)} %bitcast.170), calls=%async_computation.5 | async-start | bytes 1966080 | tf_op jit(solution)/shard_map/all_to_all | solution.py:36
  145.1 14.9 %all-to-all-done.5 = bf16[16,40,768]{2,1,0:T(8,128)(2,1)S(1)} async-done(((bf16[16,40,768]{2,1,0:T(8,128)(2,1)}), bf16[16,40,768]{2,1,0:T(8,128)(2,1)S(1)}, u32[]{:S(2)}, u32[]{:S(2)}) %all-to-all-start.5) | async-done | bytes 983072 | tf_op jit(solution)/shard_map/all_to_all | solution.py:36
  163.3 3.6 all-to-all-start.4
  167.0 24.9 %expert_forward.1 = (bf16[640,3072]{1,0:T(8,128)(2,1)}, f32[640,3072]{1,0:T(8,128)}, bf16[640,768]{1,0:T(8,128)(2,1)}) custom-call(bf16[640,768]{1,0:T(8,128)(2,1)} %bitcast.154, bf16[3072,1536]{1,0:T(8,128)(2,1)} %all-gather.5.cloned.1.call-done.weight_ref), custom_call_target="tpu_custom_call" | custom-call | tf_op jit(solution)/shard_map/expert_forward/pallas_call | solution.py:288
  192.8 7.6 %grad_expert_out.1 = bf16[3072,768]{1,0:T(8,128)(2,1)} custom-call(bf16[640,3072]{1,0:T(8,128)(2,1)} %get-tuple-element.46.hidden_ref, bf16[640,768]{1,0:T(8,128)(2,1)} %bitcast.156), custom_call_target="tpu_custom_call" | custom-call | tf_op jit(solution)/shard_map/grad_expert_out/pallas_call | solution.py:367
  200.5 14.1 %expert_backward.1 = (bf16[640,3072]{1,0:T(8,128)(2,1)}, bf16[640,1536]{1,0:T(8,128)(2,1)}) custom-call(bf16[640,768]{1,0:T(8,128)(2,1)} %bitcast.157, bf16[3072,1536]{1,0:T(8,128)(2,1)} %all-gather.5.cloned.1.call-done.weight_ref, f32[640,3072]{1,0:T(8,128)} %get-tuple-element.40.slope_ref, bf16[640,768]{1,0:T(8,128)(2,1)} %get-tuple-element.42.produced_ref), custom_call_target="tpu_custom_call" | custom-call | tf_op jit(solution)/shard_map/expert_backward/pallas_call | solution.py:335
  214.6 7.7 %grad_expert_in.1 = bf16[3072,768]{1,0:T(8,128)(2,1)} custom-call(bf16[640,3072]{1,0:T(8,128)(2,1)} %get-tuple-element.52.hidden_ref, bf16[640,768]{1,0:T(8,128)(2,1)} %bitcast.155), custom_call_target="tpu_custom_call" | custom-call | tf_op jit(solution)/shard_map/grad_expert_in/pallas_call | solution.py:367
  222.3 7.4 %all-to-all-start.6 = ((bf16[16,40,1536]{2,1,0:T(8,128)(2,1)}), bf16[16,40,1536]{2,1,0:T(8,128)(2,1)}, u32[]{:S(2)}, u32[]{:S(2)}) async-start(bf16[16,40,1536]{2,1,0:T(8,128)(2,1)} %bitcast.176), calls=%async_computation.6 | async-start | bytes 3932160 | tf_op jit(solution)/shard_map/all_to_all | solution.py:36
  230.7 26.9 %all-to-all-done.6 = bf16[16,40,1536]{2,1,0:T(8,128)(2,1)} async-done(((bf16[16,40,1536]{2,1,0:T(8,128)(2,1)}), bf16[16,40,1536]{2,1,0:T(8,128)(2,1)}, u32[]{:S(2)}, u32[]{:S(2)}) %all-to-all-start.6) | async-done | bytes 1966112 | tf_op jit(solution)/shard_map/all_to_all | solution.py:36
  257.6 3.3 fusion.6
  268.5 5.4 %all-to-all-start.7 = ((bf16[8,256,128]{2,1,0:T(8,128)(2,1)}), bf16[8,256,128]{2,1,0:T(8,128)(2,1)S(1)}, u32[]{:S(2)}, u32[]{:S(2)}) async-start(bf16[8,256,128]{2,1,0:T(8,128)(2,1)} %bitcast.146), calls=%async_computation.7 | async-start | bytes 1048576 | tf_op jit(solution)/shard_map/all_to_all | solution.py:36
  277.2 6.6 %all-to-all-done.7 = bf16[8,256,128]{2,1,0:T(8,128)(2,1)S(1)} async-done(((bf16[8,256,128]{2,1,0:T(8,128)(2,1)}), bf16[8,256,128]{2,1,0:T(8,128)(2,1)S(1)}, u32[]{:S(2)}, u32[]{:S(2)}) %all-to-all-start.7) | async-done | bytes 524320 | tf_op jit(solution)/shard_map/all_to_all | solution.py:36
  284.5 4.7 %all-to-all-start.8 = ((bf16[128,6,896]{2,1,0:T(8,128)(2,1)}), bf16[128,6,896]{2,1,0:T(8,128)(2,1)S(1)}, u32[]{:S(2)}, u32[]{:S(2)}) async-start(bf16[128,6,896]{2,1,0:T(8,128)(2,1)} %reshape.387), calls=%async_computation.8 | async-start | bytes 3670016 | tf_op jit(solution)/shard_map/all_to_all | solution.py:36
  291.6 31.2 %attention_backward.1 = (bf16[2048,384]{1,0:T(8,128)(2,1)}, f32[8,2304]{1,0:T(8,128)}) custom-call(s32[12]{0:T(128)} %pad_add_fusion.items_ref, f32[8,2304]{1,0:T(8,128)} %pad.28.bias_ref, bf16[2048,384]{1,0:T(8,128)(2,1)} %convolution_convert_fusion.qkv_ref, bf16[2048,128]{1,0:T(8,128)(2,1)} %bitcast.175, f32[2,8,1,256]{3,2,1,0:T(1,128)} %get-tuple-element.44.lse_ref), custom_call_target="tpu_custom_call" | custom-call | tf_op jit(solution)/shard_map/attention_backward/pallas_call | solution.py:222
  322.8 10.4 %all-to-all-done.8 = bf16[128,6,896]{2,1,0:T(8,128)(2,1)S(1)} async-done(((bf16[128,6,896]{2,1,0:T(8,128)(2,1)}), bf16[128,6,896]{2,1,0:T(8,128)(2,1)S(1)}, u32[]{:S(2)}, u32[]{:S(2)}) %all-to-all-start.8) | async-done | bytes 1376288 | tf_op jit(solution)/shard_map/all_to_all | solution.py:36
  334.7 4.6 %all-to-all-start.9 = ((bf16[8,256,384]{2,1,0:T(8,128)(2,1)}), bf16[8,256,384]{2,1,0:T(8,128)(2,1)}, u32[]{:S(2)}, u32[]{:S(2)}) async-start(bf16[8,256,384]{2,1,0:T(8,128)(2,1)} %bitcast.161), calls=%async_computation.10 | async-start | bytes 3145728 | tf_op jit(solution)/shard_map/all_to_all | solution.py:36
  349.9 15.9 %reduce-scatter.5.cloned.1.call-done = bf16[768,768]{1,0:T(8,128)(2,1)} async-done(((bf16[3072,768]{1,0:T(8,128)(2,1)}), bf16[768,768]{1,0:T(8,128)(2,1)}) %reduce-scatter.5.cloned.1.call-update) | async-done | bytes 1179664 | tf_op jit(solution)/shard_map/reduce_scatter | solution.py:413
  369.0 12.0 %all-to-all-start.10 = ((bf16[128,6,512]{2,1,0:T(8,128)(2,1)}), bf16[128,6,512]{2,1,0:T(8,128)(2,1)S(1)}, u32[]{:S(2)}, u32[]{:S(2)}) async-start(bf16[128,6,512]{2,1,0:T(8,128)(2,1)} %fusion.13), calls=%async_computation.11 | async-start | bytes 2097152 | tf_op jit(solution)/shard_map/all_to_all | solution.py:36
  383.6 6.2 %input_gradient.1 = f32[256,768]{1,0:T(8,128)} custom-call(s32[8]{0:T(128)} %fusion.39.places_ref, bf16[8,256,384]{2,1,0:T(8,128)(2,1)} %all-to-all-done.9.rows_ref, bf16[8,768,384]{2,1,0:T(8,128)(2,1)} %bitcast.168, f32[256,768]{1,0:T(8,128)} %copy-done.2, f32[256,768]{1,0:T(8,128)} %get-tuple-element.153.normed_ref, f32[256,1]{1,0:T(8,128)} %copy.216.factor_ref, ...), custom_call_target="tpu_custom_call" | custom-call | tf_op jit(solution)/shard_map/input_gradient/pallas_call | solution.py:392
  392.3 7.2 %all-to-all-done.10 = bf16[128,6,512]{2,1,0:T(8,128)(2,1)S(1)} async-done(((bf16[128,6,512]{2,1,0:T(8,128)(2,1)}), bf16[128,6,512]{2,1,0:T(8,128)(2,1)S(1)}, u32[]{:S(2)}, u32[]{:S(2)}) %all-to-all-start.10) | async-done | bytes 786464 | tf_op jit(solution)/shard_map/all_to_all | solution.py:36
  (243 shorter events, 72.5 us)
Async XLA Ops:
  10.7 14.4 %collective-permute-start = (bf16[256,768]{1,0:T(8,128)(2,1)S(1)}, bf16[256,768]{1,0:T(8,128)(2,1)S(1)}, u32[]{:S(2)}, u32[]{:S(2)}) collective-permute-start(bf16[256,768]{1,0:T(8,128)(2,1)S(1)} %get-tuple-element.152), channel_id=1, source_target_pairs={{0,64},{64,0},{1,65},{65,1},{2,66},{66,2},{3,67},{67,3},{4,68},{68... | collective-permute-start | bytes 1179656 | tf_op jit(solution)/shard_map/ppermute | solution.py:403
  13.9 11.1 %all-to-all-start = ((bf16[8,6,1408]{2,1,0:T(8,128)(2,1)}), bf16[8,6,1408]{2,1,0:T(8,128)(2,1)S(1)}, u32[]{:S(2)}, u32[]{:S(2)}) async-start(bf16[8,6,1408]{2,1,0:T(8,128)(2,1)} %pad.27), calls=%async_computation | async-start | bytes 360448 | tf_op jit(solution)/shard_map/all_to_all | solution.py:36
  18.2 48.6 %all-gather.9.cloned.1.call-start = ((), (), s32[]{:S(2)}) async-start(), calls=%async_computation.17 | async-start | bytes 3932160 | tf_op jit(solution)/shard_map/all_gather | solution.py:471
  25.1 42.7 %copy-start.25 = (bf16[48,1408]{1,0:T(8,128)(2,1)}, bf16[48,1408]{1,0:T(8,128)(2,1)S(1)}, u32[]{:S(2)}) copy-start(bf16[48,1408]{1,0:T(8,128)(2,1)S(1)} %reshape.368) | copy-start | bytes 405508
  26.8 29.1 %collective-permute-start.2 = (bf16[384,1536]{1,0:T(8,128)(2,1)S(1)}, bf16[384,1536]{1,0:T(8,128)(2,1)}, u32[]{:S(2)}, u32[]{:S(2)}) collective-permute-start(bf16[384,1536]{1,0:T(8,128)(2,1)S(1)} %pad_maximum_fusion.2), channel_id=1, source_target_pairs={{0,64},{64,0},{1,65},{65,1},{2,66},{66,2},{3,67},{67,3},{4,68},{68... | collective-permute-start | bytes 3538952 | tf_op jit(solution)/shard_map/ppermute | solution.py:403
  28.4 38.2 %all-to-all-start.1 = ((bf16[16,48,512]{2,1,0:T(8,128)(2,1)}), bf16[16,48,512]{2,1,0:T(8,128)(2,1)S(1)}, u32[]{:S(2)}, u32[]{:S(2)}) async-start(bf16[16,48,512]{2,1,0:T(8,128)(2,1)} %broadcast_in_dim.161), calls=%async_computation.1 | async-start | bytes 1572864 | tf_op jit(solution)/shard_map/all_to_all | solution.py:36
  36.3 130.7 %all-gather.5.cloned.1.call-start = ((), (), s32[]{:S(2)}) async-start(), calls=%async_computation.13 | async-start | bytes 11796480 | tf_op jit(solution)/shard_map/all_gather | solution.py:409
  58.7 8.2 %copy-start.34 = (s32[4]{0:T(128)S(1)}, s32[4]{0:T(128)}, u32[]{:S(2)}) copy-start(s32[4]{0:T(128)} %constant.100.clone) | copy-start | bytes 52
  58.7 8.2 %copy-start.35 = (s32[4]{0:T(128)S(1)}, s32[4]{0:T(128)}, u32[]{:S(2)}) copy-start(s32[4]{0:T(128)} %constant.99.clone) | copy-start | bytes 52
  58.7 8.8 %copy-start.28 = (s32[1,256,2]{1,2,0:T(2,128)S(1)}, s32[1,256,2]{1,2,0:T(2,128)}, u32[]{:S(2)}) copy-start(s32[1,256,2]{1,2,0:T(2,128)} %param.15) | copy-start | bytes 6148
  69.1 8.7 %copy-start.17 = (bf16[768,384]{1,0:T(8,128)(2,1)}, bf16[768,384]{1,0:T(8,128)(2,1)S(1)}, u32[]{:S(2)}) copy-start(bf16[768,384]{1,0:T(8,128)(2,1)S(1)} %slice.183) | copy-start | bytes 1769476
  70.8 37.0 %all-to-all-start.2 = ((bf16[16,48,896]{2,1,0:T(8,128)(2,1)}), bf16[16,48,896]{2,1,0:T(8,128)(2,1)S(1)}, u32[]{:S(2)}, u32[]{:S(2)}) async-start(bf16[16,48,896]{2,1,0:T(8,128)(2,1)} %broadcast_in_dim.166), calls=%async_computation.2 | async-start | bytes 2752512 | tf_op jit(solution)/shard_map/all_to_all | solution.py:36
  77.8 29.9 %collective-permute-start.1 = (bf16[768,384]{1,0:T(8,128)(2,1)S(1)}, bf16[768,384]{1,0:T(8,128)(2,1)S(1)}, u32[]{:S(2)}, u32[]{:S(2)}) collective-permute-start(bf16[768,384]{1,0:T(8,128)(2,1)S(1)} %slice.183), channel_id=1, source_target_pairs={{0,64},{64,0},{1,65},{65,1},{2,66},{66,2},{3,67},{67,3},{4,68},{68... | collective-permute-start | bytes 1769480 | tf_op jit(solution)/shard_map/ppermute | solution.py:403
  112.0 18.3 %all-to-all-start.3 = ((bf16[8,256,128]{1,2,0:T(8,128)(2,1)}), bf16[8,256,128]{1,2,0:T(8,128)(2,1)S(1)}, u32[]{:S(2)}, u32[]{:S(2)}) async-start(bf16[8,256,128]{1,2,0:T(8,128)(2,1)} %copy.207), calls=%async_computation.3 | async-start | bytes 1048576 | tf_op jit(solution)/shard_map/all_to_all | solution.py:36
  117.0 14.1 %copy-start.7 = (f32[1,256,768]{2,1,0:T(8,128)S(1)}, f32[1,256,768]{2,1,0:T(8,128)}, u32[]{:S(2)}) copy-start(f32[1,256,768]{2,1,0:T(8,128)} %param.14) | copy-start | bytes 2359300
  135.9 24.0 %all-to-all-start.5 = ((bf16[16,40,768]{2,1,0:T(8,128)(2,1)}), bf16[16,40,768]{2,1,0:T(8,128)(2,1)S(1)}, u32[]{:S(2)}, u32[]{:S(2)}) async-start(bf16[16,40,768]{2,1,0:T(8,128)(2,1)} %bitcast.170), calls=%async_computation.5 | async-start | bytes 1966080 | tf_op jit(solution)/shard_map/all_to_all | solution.py:36
  142.6 79.6 %all-gather.7.cloned.1.call-start = ((), (), s32[]{:S(2)}) async-start(), calls=%async_computation.15 | async-start | bytes 5898240 | tf_op jit(solution)/shard_map/all_gather | solution.py:409
  163.3 28.6 %all-to-all-start.4 = ((bf16[16,40,768]{2,1,0:T(8,128)(2,1)}), bf16[16,40,768]{2,1,0:T(8,128)(2,1)S(1)}, u32[]{:S(2)}, u32[]{:S(2)}) async-start(bf16[16,40,768]{2,1,0:T(8,128)(2,1)} %bitcast.177), calls=%async_computation.4 | async-start | bytes 1966080 | tf_op jit(solution)/shard_map/all_to_all | solution.py:36
  166.9 122.4 %reduce-scatter.3.cloned.1.call-start = ((), (), s32[]{:S(2)}) async-start(), calls=%async_computation.14 | async-start | bytes 5898240 | tf_op jit(solution)/shard_map/reduce_scatter | solution.py:413
  200.5 165.3 %reduce-scatter.5.cloned.1.call-start = ((), (), s32[]{:S(2)}) async-start(), calls=%async_computation.16 | async-start | bytes 5898240 | tf_op jit(solution)/shard_map/reduce_scatter | solution.py:413
  222.3 35.3 %copy-start.8 = (f32[1,256,768]{2,1,0:T(8,128)S(1)}, f32[1,256,768]{2,1,0:T(8,128)}, u32[]{:S(2)}) copy-start(f32[1,256,768]{2,1,0:T(8,128)} %param.25) | copy-start | bytes 2359300
  222.3 35.3 %all-to-all-start.6 = ((bf16[16,40,1536]{2,1,0:T(8,128)(2,1)}), bf16[16,40,1536]{2,1,0:T(8,128)(2,1)}, u32[]{:S(2)}, u32[]{:S(2)}) async-start(bf16[16,40,1536]{2,1,0:T(8,128)(2,1)} %bitcast.176), calls=%async_computation.6 | async-start | bytes 3932160 | tf_op jit(solution)/shard_map/all_to_all | solution.py:36
  268.5 15.2 %all-to-all-start.7 = ((bf16[8,256,128]{2,1,0:T(8,128)(2,1)}), bf16[8,256,128]{2,1,0:T(8,128)(2,1)S(1)}, u32[]{:S(2)}, u32[]{:S(2)}) async-start(bf16[8,256,128]{2,1,0:T(8,128)(2,1)} %bitcast.146), calls=%async_computation.7 | async-start | bytes 1048576 | tf_op jit(solution)/shard_map/all_to_all | solution.py:36
  284.5 48.7 %all-to-all-start.8 = ((bf16[128,6,896]{2,1,0:T(8,128)(2,1)}), bf16[128,6,896]{2,1,0:T(8,128)(2,1)S(1)}, u32[]{:S(2)}, u32[]{:S(2)}) async-start(bf16[128,6,896]{2,1,0:T(8,128)(2,1)} %reshape.387), calls=%async_computation.8 | async-start | bytes 3670016 | tf_op jit(solution)/shard_map/all_to_all | solution.py:36
  290.6 42.6 %collective-permute-start.3 = (bf16[384,768]{1,0:T(8,128)(2,1)S(1)}, bf16[384,768]{1,0:T(8,128)(2,1)S(1)}, u32[]{:S(2)}, u32[]{:S(2)}) collective-permute-start(bf16[384,768]{1,0:T(8,128)(2,1)S(1)} %slice.203), channel_id=1, source_target_pairs={{0,64},{64,0},{1,65},{65,1},{2,66},{66,2},{3,67},{67,3},{4,68},{68... | collective-permute-start | bytes 1769480 | tf_op jit(solution)/shard_map/ppermute | solution.py:403
  334.7 10.1 %copy-start.1 = (bf16[2048,768]{1,0:T(8,128)(2,1)S(1)}, bf16[2048,768]{1,0:T(8,128)(2,1)}, u32[]{:S(2)}) copy-start(bf16[2048,768]{1,0:T(8,128)(2,1)} %copy-done) | copy-start | bytes 9437188
  334.7 32.6 %all-to-all-start.9 = ((bf16[8,256,384]{2,1,0:T(8,128)(2,1)}), bf16[8,256,384]{2,1,0:T(8,128)(2,1)}, u32[]{:S(2)}, u32[]{:S(2)}) async-start(bf16[8,256,384]{2,1,0:T(8,128)(2,1)} %bitcast.161), calls=%async_computation.10 | async-start | bytes 3145728 | tf_op jit(solution)/shard_map/all_to_all | solution.py:36
  349.9 32.6 %copy-start.19 = (bf16[768,768]{1,0:T(8,128)(2,1)S(1)}, bf16[768,768]{1,0:T(8,128)(2,1)}, u32[]{:S(2)}) copy-start(bf16[768,768]{1,0:T(8,128)(2,1)} %reduce-scatter.3.cloned.1.call-done) | copy-start | bytes 3538948
  349.9 32.6 %copy-start.23 = (bf16[384,768]{1,0:T(8,128)(2,1)S(1)}, bf16[384,768]{1,0:T(8,128)(2,1)}, u32[]{:S(2)}) copy-start(bf16[384,768]{1,0:T(8,128)(2,1)} %copy-done.22) | copy-start | bytes 1769476
  368.3 21.4 %collective-permute-start.4 = (bf16[384,768]{1,0:T(8,128)(2,1)S(1)}, bf16[384,768]{1,0:T(8,128)(2,1)}, u32[]{:S(2)}, u32[]{:S(2)}) collective-permute-start(bf16[384,768]{1,0:T(8,128)(2,1)S(1)} %slice.162), channel_id=1, source_target_pairs={{0,64},{64,0},{1,65},{65,1},{2,66},{66,2},{3,67},{67,3},{4,68},{68... | collective-permute-start | bytes 1769480 | tf_op jit(solution)/shard_map/ppermute | solution.py:403
  369.0 30.5 %all-to-all-start.10 = ((bf16[128,6,512]{2,1,0:T(8,128)(2,1)}), bf16[128,6,512]{2,1,0:T(8,128)(2,1)S(1)}, u32[]{:S(2)}, u32[]{:S(2)}) async-start(bf16[128,6,512]{2,1,0:T(8,128)(2,1)} %fusion.13), calls=%async_computation.11 | async-start | bytes 2097152 | tf_op jit(solution)/shard_map/all_to_all | solution.py:36
  381.1 8.6 %copy-start.30 = (f32[6,17]{1,0:T(8,128)}, f32[6,17]{1,0:T(8,128)S(1)}, u32[]{:S(2)}) copy-start(f32[6,17]{1,0:T(8,128)S(1)} %slice_add_fusion.7) | copy-start | bytes 1228
  (28 other events, 94.7 us)
Sparse Core Ops, SparseCore 0:
  26.3 40.4 all-gather.8
  68.4 97.7 all-gather.4
  168.5 53.5 all-gather.6
  224.3 51.4 reduce-scatter.2
  278.1 87.5 reduce-scatter.4
